TPU v7x, 256 devices: a whole 4x4x8 slice. The times are simulated.
256 devices in a mesh: row: 8 (over y, z_lo), tm: 32 (over x, z_hi, core).
Axes of the slice: x: 4, y: 4, z: 8 (z_hi: 4, z_lo: 2; z = z_hi * 2 + z_lo), core: 2. Of those that a mesh axis runs over, the one named last changes fastest.
Arguments:
- occ_factor: float32 [32, 2048, 2048], P('tm', 'row'), may hold values from -0.077339804 to 0.077339804
- vir_factor: float32 [32, 2048, 2048], P('tm', 'row'), may hold values from -0.077339804 to 0.077339804
- eps_basis: float32 [2048, 1024], P('row'), may hold values from -0.125 to 0.125
Outputs:
- screened: float32 [32, 1024, 1024], P('tm', 'row')
All inputs are finite; a program needn't handle non-finite values.
Results may differ from a plain program's by a relative error of at most 0.000075.
Values sent between devices are 32-bit elements; how exact they have to be, the bound alone decides.
A program may use at most 128 MiB of HBM per device.

v0:
```python
import jax
import jax.numpy as jnp
from jax import lax
from jax.sharding import PartitionSpec as P

highest = lax.Precision.HIGHEST


def cut_along(x, dim, count):
    lengths = x.shape
    tiles = x.reshape(*lengths[:dim], count, lengths[dim] // count, *lengths[dim + 1 :])
    return jnp.moveaxis(tiles, dim, 0)


def sent_and_summed(x, axis, dim):
    tiles = cut_along(x, dim, lax.axis_size(axis))
    arrived = lax.all_to_all(tiles, axis, split_axis=0, concat_axis=0, tiled=True)
    return arrived.sum(axis=0)


def cosine_table(length):
    freq_index = jnp.arange(length, dtype=jnp.float32)[:, None]
    time_index = jnp.arange(length, dtype=jnp.float32)[None, :]
    table = jnp.cos(jnp.pi * freq_index * (time_index + 0.5) / length) * jnp.sqrt(2.0 / length)
    return jnp.where(freq_index == 0, table * jnp.sqrt(0.5), table)


def pair_tiles(own_occ, own_vir, far_occ, far_vir):
    occ_tile = jnp.einsum("trn,tkn->trk", own_occ, far_occ, precision=highest)
    vir_tile = jnp.einsum("trn,tkn->trk", own_vir, far_vir, precision=highest)
    return occ_tile * vir_tile


def on_device(occ_factor, vir_factor, eps_basis):
    local_times = occ_factor.shape[0]
    time_total = local_times * lax.axis_size("tm")
    table = cosine_table(time_total)
    far_occ = lax.all_gather(occ_factor, "row", axis=1, tiled=True)
    far_vir = lax.all_gather(vir_factor, "row", axis=1, tiled=True)
    far_basis = lax.all_gather(eps_basis[None], "row", axis=1, tiled=True)
    polar = pair_tiles(occ_factor, vir_factor, far_occ, far_vir)
    payload = jnp.einsum("trk,ke->tre", polar, far_basis[0], precision=highest)
    partial_terms = jnp.einsum("re,tro->teo", eps_basis, payload, precision=highest)
    owned = sent_and_summed(partial_terms, "row", 1)
    frequency_block = jnp.einsum(
        "kt,tic->kic",
        table,
        lax.all_to_all(owned, "tm", split_axis=2, concat_axis=0, tiled=True),
        precision=highest,
    )
    return lax.all_to_all(frequency_block, "tm", split_axis=0, concat_axis=2, tiled=True)


def solution(mesh):
    placed = (P("tm", "row", None), P("tm", "row", None), P("row", None))
    return jax.shard_map(
        on_device, mesh=mesh, in_specs=placed, out_specs=P("tm", "row", None), check_vma=False
    )
```

profile of v0, /device:TPU:1, one launch (start us, length us, event | category | flops | bytes accessed | tf_op | source)
XLA Modules:
  0.0 976.1 jit_solution(13410359877314354971)
XLA Ops:
  6.5 0.0 all-gather.7.cloned.1.call-start
  6.5 0.0 copy-start
  6.5 0.7 all-gather.7.cloned.1.call-update
  7.3 0.0 all-gather.5.cloned.1.call-start
  7.3 0.7 all-gather.5.cloned.1.call-update
  8.0 0.0 all-gather.9.cloned.1.call-start
  8.1 0.7 all-gather.9.cloned.1.call-update
  8.7 332.5 %all-gather.7.cloned.1.call-done = f32[1,2048,2048]{2,1,0:T(8,128)} async-done(((f32[1,256,2048]{2,1,0:T(8,128)}), f32[1,2048,2048]{2,1,0:T(8,128)}) %all-gather.7.cloned.1.call-update) | async-done | bytes 16777232 | tf_op jit(solution)/shard_map/all_gather | solution.py:39
  341.2 0.0 copy-done
  341.2 17.8 %fusion = f32[256,2048]{1,0:T(8,128)} fusion(f32[1,2048,2048]{2,1,0:T(8,128)} %all-gather.7.cloned.1.call-done, f32[1,256,2048]{2,1,0:T(8,128)S(1)} %copy-done), kind=kOutput, calls=%fused_computation | convolution fusion | flops 12884901888 | bytes 20971520 | tf_op jit(solution)/shard_map/trn,tkn->trk/dot_general | solution.py:30
  359.1 313.2 %all-gather.5.cloned.1.call-done = f32[1,2048,2048]{2,1,0:T(8,128)} async-done(((f32[1,256,2048]{2,1,0:T(8,128)}), f32[1,2048,2048]{2,1,0:T(8,128)}) %all-gather.5.cloned.1.call-update) | async-done | bytes 16777232 | tf_op jit(solution)/shard_map/all_gather | solution.py:38
  672.3 17.9 %fusion.4 = f32[256,2048]{1,0:T(8,128)S(1)} fusion(f32[256,2048]{1,0:T(8,128)} %fusion, f32[1,2048,2048]{2,1,0:T(8,128)} %all-gather.5.cloned.1.call-done, f32[1,256,2048]{2,1,0:T(8,128)} %param.3), kind=kOutput, calls=%fused_computation.5 | convolution fusion | flops 12885426176 | bytes 23068672 | tf_op jit(solution)/shard_map/trn,tkn->trk/dot_general | solution.py:29
  690.1 0.0 copy-start.1
  690.1 155.9 %all-gather.9.cloned.1.call-done = f32[2048,1024]{1,0:T(8,128)} async-done(((f32[256,1024]{1,0:T(8,128)}), f32[2048,1024]{1,0:T(8,128)}) %all-gather.9.cloned.1.call-update) | async-done | bytes 8388624 | tf_op jit(solution)/shard_map/all_gather | solution.py:40
  846.0 10.0 %fusion.28 = f32[256,1024]{1,0:T(8,128)S(1)} fusion(f32[256,2048]{1,0:T(8,128)S(1)} %fusion.4, f32[2048,1024]{1,0:T(8,128)} %all-gather.9.cloned.1.call-done), kind=kOutput, calls=%fused_computation.30 | convolution fusion | flops 6442450944 | bytes 11534336 | tf_op jit(solution)/shard_map/trk,ke->tre/dot_general | solution.py:42
  856.0 0.0 copy-done.1
  856.0 3.8 fusion.29
  859.8 53.5 %all_to_all.41 = f32[8,1,128,1024]{3,2,1,0:T(8,128)S(1)} all-to-all(f32[8,1,128,1024]{3,2,1,0:T(8,128)S(1)} %bitcast.42), channel_id=1, replica_groups=mesh['row'=8,'tm'=32] {'row'}, dimensions={0} | all-to-all | bytes 8388608 | tf_op jit(solution)/shard_map/all_to_all | solution.py:17
  913.3 0.4 bitcast_reduce_fusion
  913.7 1.0 copy.9
  914.8 11.5 %all-to-all-start.1 = ((f32[1,128,1024]{1,0,2:T(1,128)}), f32[1,128,1024]{1,0,2:T(1,128)S(1)}, u32[]{:S(2)}, u32[]{:S(2)}) async-start(f32[1,128,1024]{1,0,2:T(1,128)} %copy.9), calls=%async_computation.1 | async-start | bytes 1048576 | tf_op jit(solution)/shard_map/all_to_all | solution.py:48
  926.3 17.9 %all-to-all-done.1 = f32[1,128,1024]{1,0,2:T(1,128)S(1)} async-done(((f32[1,128,1024]{1,0,2:T(1,128)}), f32[1,128,1024]{1,0,2:T(1,128)S(1)}, u32[]{:S(2)}, u32[]{:S(2)}) %all-to-all-start.1) | async-done | bytes 524320 | tf_op jit(solution)/shard_map/all_to_all | solution.py:48
  944.2 1.0 fusion.9
  945.2 0.3 copy.11
  945.5 23.1 %all_to_all.42 = f32[32,128,32]{1,2,0:T(8,128)S(1)} all-to-all(f32[32,128,32]{1,2,0:T(8,128)S(1)} %copy.11), channel_id=1, replica_groups=mesh['row'=8,'tm'=32] {'tm'}, dimensions={0} | all-to-all | bytes 1048576 | tf_op jit(solution)/shard_map/all_to_all | solution.py:51
  968.6 1.0 copy.12
  (2 shorter events, 0.0 us)
Async XLA Ops:
  6.5 334.7 %all-gather.7.cloned.1.call-start = ((), (), s32[]{:S(2)}) async-start(), calls=%async_computation.4 | async-start | bytes 18874368 | tf_op jit(solution)/shard_map/all_gather | solution.py:39
  6.5 334.7 %copy-start = (f32[1,256,2048]{2,1,0:T(8,128)S(1)}, f32[1,256,2048]{2,1,0:T(8,128)}, u32[]{:S(2)}) copy-start(f32[1,256,2048]{2,1,0:T(8,128)} %param.4) | copy-start | bytes 6291460
  7.3 665.0 %all-gather.5.cloned.1.call-start = ((), (), s32[]{:S(2)}) async-start(), calls=%async_computation.3 | async-start | bytes 18874368 | tf_op jit(solution)/shard_map/all_gather | solution.py:38
  8.0 838.0 %all-gather.9.cloned.1.call-start = ((), (), s32[]{:S(2)}) async-start(), calls=%async_computation.5 | async-start | bytes 9437184 | tf_op jit(solution)/shard_map/all_gather | solution.py:40
  690.1 165.9 %copy-start.1 = (f32[256,1024]{1,0:T(8,128)S(1)}, f32[256,1024]{1,0:T(8,128)}, u32[]{:S(2)}) copy-start(f32[256,1024]{1,0:T(8,128)} %param.5) | copy-start | bytes 3145732
  914.8 29.4 %all-to-all-start.1 = ((f32[1,128,1024]{1,0,2:T(1,128)}), f32[1,128,1024]{1,0,2:T(1,128)S(1)}, u32[]{:S(2)}, u32[]{:S(2)}) async-start(f32[1,128,1024]{1,0,2:T(1,128)} %copy.9), calls=%async_computation.1 | async-start | bytes 1048576 | tf_op jit(solution)/shard_map/all_to_all | solution.py:48
Sparse Core Ops, SparseCore 0:
  9.1 332.0 all-gather.6
  343.0 329.2 all-gather.4
  674.1 171.9 all-gather.8
where the time goes:
time: 976 us
  waiting for transfers between devices  822 us (84%)
  blocking collectives  76.6 us (8%)
  matrix products  50.5 us (5%)
  between operations  13.2 us (1%)
  starting transfers between devices  11.5 us (1%)
    all_gather x1, waiting for transfers between devices, on_device(): far_vir = lax.all_gather(vir_factor, 'row', axis=1, tiled=True)  332 us
    all_gather x1, waiting for transfers between devices, on_device(): far_occ = lax.all_gather(occ_factor, 'row', axis=1, tiled=True)  313 us
    all_gather x1, waiting for transfers between devices, on_device(): far_basis = lax.all_gather(eps_basis[None], 'row', axis=1, tiled=True)  156 us
    all_to_all x1, blocking collectives, sent_and_summed(): lax.all_to_all(tiles, axis, split_axis=0, concat_axis=0, tiled=True)  53.5 us
    all_to_all x1, blocking collectives, on_device(): lax.all_to_all(frequency_block, 'tm', split_axis=0, concat_axis=2, tiled=...  23.1 us
  transfers between devices with their start and end apart: 4, of which 4 were waited for; matrix products, arithmetic and copies ran while one was open for 4% of the time, Pallas kernels for 0%

commit v1 on v0

v1 whole, which is shorter than its diff:
```python
import functools
import math

import jax
import jax.numpy as jnp
from jax import lax
from jax.experimental import pallas as pl
from jax.experimental.pallas import tpu as pltpu
from jax.sharding import PartitionSpec as P

F32 = jnp.float32
BF16 = jnp.bfloat16
NT_DIMS = (((1,), (1,)), ((), ()))
NN_DIMS = (((1,), (0,)), ((), ()))
TN_DIMS = (((0,), (0,)), ((), ()))
NEXT, OWN, ACROSS, FAR = 0, 1, 2, 3
ROWS = 256
HALF = 128
TILE = 128


def halves_of(x):
    high = x.astype(BF16)
    return high, (x - high.astype(F32)).astype(BF16)


def dot3(lhs, rhs, dims):
    mul = functools.partial(lax.dot_general, dimension_numbers=dims, preferred_element_type=F32)
    return mul(lhs[0], rhs[0]) + (mul(lhs[0], rhs[1]) + mul(lhs[1], rhs[0]))


def green_kernel(
    occ, vir, eps, out, full, high, low, basis, basis_high, basis_low, polar, total, staged, arrived,
    local_sem, basis_send, basis_recv, send, recv, part_send, part_recv,
):
    row, tm = lax.axis_index("row"), lax.axis_index("tm")
    y, z = lax.div(row, 2), lax.rem(row, 2)
    step = 1 - 2 * lax.rem(tm, 2)
    before = {"row": lax.rem(y - step + 4, 4) * 2 + z, "tm": tm}
    across = {"row": y * 2 + 1 - z, "tm": tm}

    barrier = pltpu.get_barrier_semaphore()

    def greet(i, carry):
        pl.semaphore_signal(barrier, inc=1, device_id={"row": lax.rem(row + i, 8), "tm": tm})
        return carry

    lax.fori_loop(1, 8, greet, 0)
    pl.semaphore_wait(barrier, 7)

    def block(slot, chunk=None):
        if chunk is None:
            return pl.ds(slot * ROWS, ROWS)
        return pl.ds(slot * ROWS + chunk * HALF, HALF)

    def send_basis(src, slot, device):
        return pltpu.make_async_remote_copy(
            src, basis.at[block(slot)], basis_send.at[slot], basis_recv.at[slot], device_id=device
        )

    def send_rows(which, chunk, src, slot, device):
        return pltpu.make_async_remote_copy(
            src, full.at[which, block(slot, chunk)],
            send.at[which, slot, chunk], recv.at[which, slot, chunk], device_id=device,
        )

    sources = (occ.at[0], vir.at[0])
    copies = {}
    copies["basis", NEXT] = send_basis(eps, NEXT, before)
    copies["basis", ACROSS] = send_basis(eps, ACROSS, across)
    for chunk in range(2):
        for which in range(2):
            part = sources[which].at[pl.ds(chunk * HALF, HALF)]
            copies[which, NEXT, chunk] = send_rows(which, chunk, part, NEXT, before)
            copies[which, ACROSS, chunk] = send_rows(which, chunk, part, ACROSS, across)
    for copy in copies.values():
        copy.start()

    own = [pltpu.make_async_copy(sources[which], full.at[which, block(OWN)], local_sem.at[which]) for which in range(2)]
    own.append(pltpu.make_async_copy(eps, basis.at[block(OWN)], local_sem.at[2]))
    for copy in own:
        copy.start()
    for copy in own:
        copy.wait()

    def convert(slot, chunk):
        start = slot * ROWS + chunk * HALF

        def body(i, carry):
            rows = pl.ds(start + i * 16, 16)
            for which in range(2):
                high[which, rows], low[which, rows] = halves_of(full[which, rows])
            return carry

        lax.fori_loop(0, HALF // 16, body, 0)

    def convert_basis(slot):
        def body(i, carry):
            rows = pl.ds(slot * ROWS + i * 16, 16)
            basis_high[rows], basis_low[rows] = halves_of(basis[rows])
            return carry

        lax.fori_loop(0, ROWS // 16, body, 0)

    def greens(left, right, width, weight):
        def one(which):
            lhs = (high[which, pl.ds(left, HALF)], low[which, pl.ds(left, HALF)])
            rhs = (high[which, pl.ds(right, width)], low[which, pl.ds(right, width)])
            return dot3(lhs, rhs, NT_DIMS)

        polar[:, pl.ds(right, width)] = weight * (one(0) * one(1))

    def project(left, spans, first):
        term = None
        for start, width in spans:
            rhs = (basis_high[pl.ds(start, width)], basis_low[pl.ds(start, width)])
            new = dot3(halves_of(polar[:, pl.ds(start, width)]), rhs, NN_DIMS)
            term = new if term is None else term + new
        term = halves_of(term)

        def body(i, carry):
            columns = pl.ds(pl.multiple_of(i * 256, 256), 256)
            lhs = (basis_high[pl.ds(left, HALF), columns], basis_low[pl.ds(left, HALF), columns])
            new = dot3(lhs, term, TN_DIMS)
            total[columns] = new if first else total[columns] + new
            return carry

        lax.fori_loop(0, 4, body, 0)

    def at(slot, chunk=0):
        return slot * ROWS + chunk * HALF

    def wait_rows(slot, chunk):
        for which in range(2):
            copies[which, slot, chunk].wait_recv()

    def work(slot, chunk, spans, first=False):
        for start, width, weight in spans:
            greens(at(slot, chunk), start, width, weight)
        project(at(slot, chunk), [span[:2] for span in spans], first)

    convert_basis(OWN)
    for chunk in range(2):
        convert(OWN, chunk)
    work(OWN, 0, [(at(OWN), ROWS, 0.5)], first=True)
    work(OWN, 1, [(at(OWN), ROWS, 0.5)])

    copies["basis", NEXT].wait_recv()
    copies["basis", FAR] = send_basis(basis.at[block(NEXT)], FAR, before)
    copies["basis", FAR].start()
    convert_basis(NEXT)
    for chunk in range(2):
        wait_rows(NEXT, chunk)
        for which in range(2):
            copies[which, FAR, chunk] = send_rows(which, chunk, full.at[which, block(NEXT, chunk)], FAR, before)
            copies[which, FAR, chunk].start()
        convert(NEXT, chunk)
        work(NEXT, chunk, [(at(OWN), ROWS, 1.0)])

    copies["basis", ACROSS].wait_recv()
    convert_basis(ACROSS)
    wait_rows(ACROSS, 0)
    convert(ACROSS, 0)
    work(ACROSS, 0, [(at(NEXT), ROWS, 1.0), (at(OWN), ROWS, 0.5)])
    copies["basis", FAR].wait_recv()
    convert_basis(FAR)
    wait_rows(FAR, 0)
    convert(FAR, 0)
    work(FAR, 0, [(at(OWN), ROWS, 0.5), (at(ACROSS), HALF, 0.5)])
    wait_rows(ACROSS, 1)
    convert(ACROSS, 1)
    work(ACROSS, 1, [(at(NEXT), ROWS, 1.0), (at(OWN), ROWS, 0.5), (at(FAR), HALF, 0.5)])
    wait_rows(FAR, 1)
    convert(FAR, 1)
    work(FAR, 1, [(at(OWN), ROWS, 0.5), (at(ACROSS), ROWS, 0.5)])

    def fold(owner, slot):
        rows = pl.ds(pl.multiple_of(owner * TILE, TILE), TILE)
        for j in range(8):
            tile = pl.ds(j * TILE, TILE)
            staged[slot, tile] = total[rows, tile] + total[tile, rows].T

    def part_copy(owner, i):
        return pltpu.make_async_remote_copy(
            staged.at[i], arrived.at[i], part_send.at[i], part_recv.at[i],
            device_id={"row": owner, "tm": tm},
        )

    def send_part(i, carry):
        owner = lax.rem(row + i, 8)
        fold(owner, i)
        part_copy(owner, i).start()
        return carry

    lax.fori_loop(1, 8, send_part, 0)
    fold(row, 0)

    def take_part(i, carry):
        part_copy(row, i).wait_recv()
        return carry

    lax.fori_loop(1, 8, take_part, 0)

    def add(i, carry):
        rows = pl.ds(i * 64, 64)
        value = staged[0, rows]
        for j in range(1, 8):
            value = value + arrived[j, rows]
        out[rows] = value
        return carry

    lax.fori_loop(0, 16, add, 0)

    for copy in copies.values():
        copy.wait_send()

    def drain(i, carry):
        part_copy(row, i).wait_send()
        return carry

    lax.fori_loop(1, 8, drain, 0)


def green_sums(occ, vir, eps):
    dma = pltpu.SemaphoreType.DMA
    return pl.pallas_call(
        green_kernel,
        out_shape=jax.ShapeDtypeStruct((1024, TILE), F32),
        in_specs=[pl.BlockSpec(memory_space=pl.ANY)] * 3,
        out_specs=pl.BlockSpec(memory_space=pltpu.VMEM),
        scratch_shapes=[
            pltpu.VMEM((2, 4 * ROWS, 2048), F32),
            pltpu.VMEM((2, 4 * ROWS, 2048), BF16),
            pltpu.VMEM((2, 4 * ROWS, 2048), BF16),
            pltpu.VMEM((4 * ROWS, 1024), F32),
            pltpu.VMEM((4 * ROWS, 1024), BF16),
            pltpu.VMEM((4 * ROWS, 1024), BF16),
            pltpu.VMEM((HALF, 4 * ROWS), F32),
            pltpu.VMEM((1024, 1024), F32),
            pltpu.VMEM((8, 1024, TILE), F32),
            pltpu.VMEM((8, 1024, TILE), F32),
            dma((3,)), dma((4,)), dma((4,)), dma((2, 4, 2)), dma((2, 4, 2)), dma((8,)), dma((8,)),
        ],
        compiler_params=pltpu.CompilerParams(
            collective_id=0, has_side_effects=True, vmem_limit_bytes=62 << 20
        ),
        cost_estimate=pl.CostEstimate(flops=20 * 10**9, bytes_accessed=20 << 20, transcendentals=0),
        name="green_sums",
    )(occ, vir, eps)


def cosine(freq, time):
    scale = math.sqrt((1.0 if freq == 0 else 2.0) / 32)
    return scale * math.cos(math.pi * freq * (time + 0.5) / 32)


def cosine_kernel(
    block, out, paired, times, freqs, gathered, final,
    core_send, core_recv, chip_send, chip_recv, back_send, back_recv, end_send, end_recv,
):
    row, tm = lax.axis_index("row"), lax.axis_index("tm")
    chip, core = lax.div(tm, 2), lax.rem(tm, 2)
    partner = {"row": row, "tm": chip * 2 + 1 - core}

    def other(i):
        return lax.rem(lax.div(chip, 4) + lax.div(i, 4), 4) * 4 + lax.rem(lax.rem(chip, 4) + lax.rem(i, 4), 4)

    barrier = pltpu.get_barrier_semaphore()

    def greet(i, carry):
        pl.semaphore_signal(barrier, inc=1, device_id={"row": row, "tm": other(i) * 2 + core})
        return carry

    lax.fori_loop(1, 16, greet, 0)
    pl.semaphore_signal(barrier, inc=1, device_id=partner)
    pl.semaphore_wait(barrier, 16)

    swap = pltpu.make_async_remote_copy(
        block.at[pl.ds(pl.multiple_of((1 - core) * 512, 512), 512)], paired.at[core],
        core_send, core_recv, device_id=partner,
    )
    swap.start()
    paired[core] = block[pl.ds(pl.multiple_of(core * 512, 512), 512)]
    swap.wait()

    def spread(i, carry):
        target = other(i)
        pltpu.make_async_remote_copy(
            paired.at[:, pl.ds(pl.multiple_of(target * 32, 32), 32)], times.at[chip],
            chip_send, chip_recv, device_id={"row": row, "tm": target * 2 + core},
        ).start()
        return carry

    lax.fori_loop(1, 16, spread, 0)
    times[chip] = paired[:, pl.ds(pl.multiple_of(chip * 32, 32), 32)]
    pltpu.make_async_copy(times.at[pl.ds(0, 15)], times.at[pl.ds(0, 15)], chip_recv).wait()

    def transform(i, carry):
        rows = pl.ds(pl.multiple_of(i * 8, 8), 8)
        at = [times[t // 2, t % 2, rows] for t in range(32)]
        mixed = ([at[t] + at[31 - t] for t in range(16)], [at[t] - at[31 - t] for t in range(16)])
        for freq in range(32):
            value = None
            for t in range(16):
                term = cosine(freq, t) * mixed[freq % 2][t]
                value = term if value is None else value + term
            freqs[freq // 2, freq % 2, rows] = value
        return carry

    lax.fori_loop(0, 4, transform, 0)

    def give(i, carry):
        target = other(i)
        pltpu.make_async_remote_copy(
            freqs.at[target], gathered.at[chip],
            back_send, back_recv, device_id={"row": row, "tm": target * 2 + core},
        ).start()
        return carry

    lax.fori_loop(1, 16, give, 0)
    gathered[chip] = freqs[chip]
    pltpu.make_async_copy(gathered.at[pl.ds(0, 15)], gathered.at[pl.ds(0, 15)], back_recv).wait()

    last = pltpu.make_async_remote_copy(
        gathered.at[:, 1 - core], final.at[core], end_send, end_recv, device_id=partner
    )
    last.start()
    final[core] = gathered[:, core]
    last.wait()
    for j in range(8):
        for part in range(4):
            out[0, part * 32:(part + 1) * 32, j * TILE:(j + 1) * TILE] = final[j // 4, (j % 4) * 4 + part]

    pltpu.make_async_copy(times.at[pl.ds(0, 15)], times.at[pl.ds(0, 15)], chip_send).wait()
    pltpu.make_async_copy(times.at[pl.ds(0, 15)], times.at[pl.ds(0, 15)], back_send).wait()


def cosine_sums(block):
    dma = pltpu.SemaphoreType.DMA
    return pl.pallas_call(
        cosine_kernel,
        out_shape=jax.ShapeDtypeStruct((1, TILE, 1024), F32),
        in_specs=[pl.BlockSpec(memory_space=pltpu.VMEM)],
        out_specs=pl.BlockSpec(memory_space=pltpu.VMEM),
        scratch_shapes=[
            pltpu.VMEM((2, 512, TILE), F32),
            pltpu.VMEM((16, 2, 32, TILE), F32),
            pltpu.VMEM((16, 2, 32, TILE), F32),
            pltpu.VMEM((16, 2, 32, TILE), F32),
            pltpu.VMEM((2, 16, 32, TILE), F32),
            dma, dma, dma, dma, dma, dma, dma, dma,
        ],
        compiler_params=pltpu.CompilerParams(
            collective_id=1, has_side_effects=True, vmem_limit_bytes=16 << 20
        ),
        cost_estimate=pl.CostEstimate(flops=10**7, bytes_accessed=1 << 20, transcendentals=0),
        name="cosine_sums",
    )(block)


def on_device(occ_factor, vir_factor, eps_basis):
    return cosine_sums(green_sums(occ_factor, vir_factor, eps_basis))


def solution(mesh):
    placed = (P("tm", "row", None), P("tm", "row", None), P("row", None))
    return jax.shard_map(
        on_device, mesh=mesh, in_specs=placed, out_specs=P("tm", "row", None), check_vma=False
    )
```

time: 976 us -> 226 us (0.23)
  waiting for transfers between devices: 822 us -> 0 us
  Pallas kernels: 0 us -> 224 us
  blocking collectives: 76.6 us -> 0 us
  matrix products: 50.5 us -> 0 us
  between operations: 13.2 us -> 0.03 us
  starting transfers between devices: 11.5 us -> 0 us
    all_gather x3 -> x0, waiting for transfers between devices: 802 us -> none  [the longest x1 332 us: on_device(): far_vir = lax.all_gather(vir_factor, 'row', axis=1, tiled=True)]
    pallas_call x0 -> x2, Pallas kernels: none -> 224 us  [the longest x1 181 us: green_sums(): pl.pallas_call(green_kernel, out_shape=jax.ShapeDtypeStruct((1024, TILE),...]
    all_to_all x2 -> x0, blocking collectives: 76.6 us -> none  [the longest x1 53.5 us: sent_and_summed(): lax.all_to_all(tiles, axis, split_axis=0, concat_axis=0, tiled=True)]
    dot_general x5 -> x0, matrix products: 50.5 us -> none  [the longest x1 17.9 us: pair_tiles(): occ_tile = jnp.einsum('trn,tkn->trk', own_occ, far_occ, precision=highest)]
    all_to_all x1 -> x0, waiting for transfers between devices: 17.9 us -> none  [on_device(): lax.all_to_all(owned, 'tm', split_axis=2, concat_axis=0, tiled=True)]
    all_to_all x1 -> x0, starting transfers between devices: 11.5 us -> none  [on_device(): lax.all_to_all(owned, 'tm', split_axis=2, concat_axis=0, tiled=True)]
  transfers between devices with their start and end apart: 4 -> 0, of which waited for: 4 -> 0; matrix products, arithmetic and copies ran while one was open for 4% -> 0% of each run, Pallas kernels for 0% -> 0%
where the time goes in v1:
time: 226 us
  Pallas kernels  224 us (99%)
    pallas_call x1, Pallas kernels, green_sums(): pl.pallas_call(green_kernel, out_shape=jax.ShapeDtypeStruct((1024, TILE),...  181 us
    pallas_call x1, Pallas kernels, cosine_sums(): pl.pallas_call(cosine_kernel, out_shape=jax.ShapeDtypeStruct((1, TILE, 10...  42.7 us

profile of v1, /device:TPU:1, one launch (start us, length us, event | category | flops | bytes accessed | tf_op | source)
XLA Modules:
  0.0 226.0 jit_solution(17097169618257727558)
XLA Ops:
  0.0 181.4 %green_sums.1.block = f32[1024,128]{1,0:T(8,128)} custom-call(f32[1,256,2048]{2,1,0:T(8,128)} %occ.1, f32[1,256,2048]{2,1,0:T(8,128)} %vir.1, f32[256,1024]{1,0:T(8,128)} %eps.1), custom_call_target="tpu_custom_call" | custom-call | flops 20000000000 | bytes 20971520 | tf_op jit(solution)/shard_map/green_sums/pallas_call | solution.py:226
  181.4 0.0 copy-start
  181.5 1.0 copy-done
  182.5 42.7 %cosine_sums.1 = f32[1,128,1024]{2,1,0:T(8,128)S(1)} custom-call(f32[1024,128]{1,0:T(8,128)S(1)} %copy-done), custom_call_target="tpu_custom_call" | custom-call | flops 10000000 | bytes 1048576 | tf_op jit(solution)/shard_map/cosine_sums/pallas_call | solution.py:340
  225.2 0.8 copy.5
Async XLA Ops:
  181.4 1.0 copy-start

commit v2 on v1

--- a/solution.py
+++ b/solution.py
@@ -17,6 +17,10 @@
 ROWS = 256
 HALF = 128
 TILE = 128
+QUARTER = 64
+KEPT = 4 * TILE + 64
+SHARE = KEPT // 2
+MAIN = 256
 
 
 def halves_of(x):
@@ -30,14 +34,16 @@
 
 
 def green_kernel(
-    occ, vir, eps, out, full, high, low, basis, basis_high, basis_low, polar, total, staged, arrived,
-    local_sem, basis_send, basis_recv, send, recv, part_send, part_recv,
+    occ, vir, eps, out, full, high, low, basis, basis_high, basis_low, polar, total, turned, staged, arrived,
+    local_sem, basis_send, basis_recv, share_send, share_recv, send, recv, part_send, part_recv,
 ):
     row, tm = lax.axis_index("row"), lax.axis_index("tm")
     y, z = lax.div(row, 2), lax.rem(row, 2)
     step = 1 - 2 * lax.rem(tm, 2)
     before = {"row": lax.rem(y - step + 4, 4) * 2 + z, "tm": tm}
     across = {"row": y * 2 + 1 - z, "tm": tm}
+    x = lax.div(tm, 8)
+    beside = [{"row": row, "tm": lax.rem(tm + 8 * i, 32)} for i in range(4)]
 
     barrier = pltpu.get_barrier_semaphore()
 
@@ -46,17 +52,36 @@
         return carry
 
     lax.fori_loop(1, 8, greet, 0)
-    pl.semaphore_wait(barrier, 7)
+    for i in range(1, 4):
+        pl.semaphore_signal(barrier, inc=1, device_id=beside[i])
+    pl.semaphore_wait(barrier, 10)
 
     def block(slot, chunk=None):
         if chunk is None:
             return pl.ds(slot * ROWS, ROWS)
         return pl.ds(slot * ROWS + chunk * HALF, HALF)
 
+    def quarter(slot, of):
+        return pl.ds(pl.multiple_of(slot * ROWS + of * QUARTER, QUARTER), QUARTER)
+
     def send_basis(src, slot, device):
         return pltpu.make_async_remote_copy(
-            src, basis.at[block(slot)], basis_send.at[slot], basis_recv.at[slot], device_id=device
+            src, basis.at[quarter(slot, x)], basis_send.at[slot], basis_recv.at[slot], device_id=device
         )
+
+    def share_basis(slot):
+        copies["basis", slot].wait_recv()
+        part = basis.at[quarter(slot, x)]
+        for i in range(1, 4):
+            copies["share", slot, i] = pltpu.make_async_remote_copy(
+                part, part, share_send.at[slot, i], share_recv.at[slot, i], device_id=beside[i]
+            )
+            copies["share", slot, i].start()
+
+    def take_basis(slot):
+        for i in range(1, 4):
+            copies["share", slot, i].wait_recv()
+        convert_basis(slot)
 
     def send_rows(which, chunk, src, slot, device):
         return pltpu.make_async_remote_copy(
@@ -66,8 +91,8 @@
 
     sources = (occ.at[0], vir.at[0])
     copies = {}
-    copies["basis", NEXT] = send_basis(eps, NEXT, before)
-    copies["basis", ACROSS] = send_basis(eps, ACROSS, across)
+    copies["basis", NEXT] = send_basis(eps.at[quarter(0, x)], NEXT, before)
+    copies["basis", ACROSS] = send_basis(eps.at[quarter(0, x)], ACROSS, across)
     for chunk in range(2):
         for which in range(2):
             part = sources[which].at[pl.ds(chunk * HALF, HALF)]
@@ -140,15 +165,19 @@
         project(at(slot, chunk), [span[:2] for span in spans], first)
 
     convert_basis(OWN)
+    share_basis(NEXT)
+    copies["basis", FAR] = send_basis(basis.at[quarter(NEXT, x)], FAR, before)
+    copies["basis", FAR].start()
+    share_basis(ACROSS)
     for chunk in range(2):
         convert(OWN, chunk)
     work(OWN, 0, [(at(OWN), ROWS, 0.5)], first=True)
     work(OWN, 1, [(at(OWN), ROWS, 0.5)])
-
-    copies["basis", NEXT].wait_recv()
-    copies["basis", FAR] = send_basis(basis.at[block(NEXT)], FAR, before)
-    copies["basis", FAR].start()
-    convert_basis(NEXT)
+    share_basis(FAR)
+    take_basis(NEXT)
+    take_basis(ACROSS)
+    take_basis(FAR)
+
     for chunk in range(2):
         wait_rows(NEXT, chunk)
         for which in range(2):
@@ -157,13 +186,9 @@
         convert(NEXT, chunk)
         work(NEXT, chunk, [(at(OWN), ROWS, 1.0)])
 
-    copies["basis", ACROSS].wait_recv()
-    convert_basis(ACROSS)
     wait_rows(ACROSS, 0)
     convert(ACROSS, 0)
     work(ACROSS, 0, [(at(NEXT), ROWS, 1.0), (at(OWN), ROWS, 0.5)])
-    copies["basis", FAR].wait_recv()
-    convert_basis(FAR)
     wait_rows(FAR, 0)
     convert(FAR, 0)
     work(FAR, 0, [(at(OWN), ROWS, 0.5), (at(ACROSS), HALF, 0.5)])
@@ -175,10 +200,19 @@
     work(FAR, 1, [(at(OWN), ROWS, 0.5), (at(ACROSS), ROWS, 0.5)])
 
     def fold(owner, slot):
-        rows = pl.ds(pl.multiple_of(owner * TILE, TILE), TILE)
-        for j in range(8):
-            tile = pl.ds(j * TILE, TILE)
-            staged[slot, tile] = total[rows, tile] + total[tile, rows].T
+        def span(j):
+            return pl.ds(pl.multiple_of(j * TILE, TILE), TILE)
+
+        rows = span(owner)
+        for d in range(4):
+            tile = span(lax.rem(owner + d, 8))
+            staged[slot, d * TILE:(d + 1) * TILE] = total[rows, tile] + total[tile, rows].T
+        low_tile, upper = lax.rem(owner, 4), lax.div(owner, 4)
+        turned[...] = total[span(low_tile + 4), span(low_tile)].T
+        half = pl.ds(pl.multiple_of(low_tile * TILE + upper * 64, 64), 64)
+        staged[slot, 4 * TILE:KEPT] = (
+            total[half, span(low_tile + 4)] + turned[pl.ds(pl.multiple_of(upper * 64, 64), 64)]
+        )
 
     def part_copy(owner, i):
         return pltpu.make_async_remote_copy(
@@ -209,7 +243,7 @@
         out[rows] = value
         return carry
 
-    lax.fori_loop(0, 16, add, 0)
+    lax.fori_loop(0, KEPT // 64, add, 0)
 
     for copy in copies.values():
         copy.wait_send()
@@ -225,7 +259,7 @@
     dma = pltpu.SemaphoreType.DMA
     return pl.pallas_call(
         green_kernel,
-        out_shape=jax.ShapeDtypeStruct((1024, TILE), F32),
+        out_shape=jax.ShapeDtypeStruct((KEPT, TILE), F32),
         in_specs=[pl.BlockSpec(memory_space=pl.ANY)] * 3,
         out_specs=pl.BlockSpec(memory_space=pltpu.VMEM),
         scratch_shapes=[
@@ -237,9 +271,10 @@
             pltpu.VMEM((4 * ROWS, 1024), BF16),
             pltpu.VMEM((HALF, 4 * ROWS), F32),
             pltpu.VMEM((1024, 1024), F32),
-            pltpu.VMEM((8, 1024, TILE), F32),
-            pltpu.VMEM((8, 1024, TILE), F32),
-            dma((3,)), dma((4,)), dma((4,)), dma((2, 4, 2)), dma((2, 4, 2)), dma((8,)), dma((8,)),
+            pltpu.VMEM((TILE, TILE), F32),
+            pltpu.VMEM((8, KEPT, TILE), F32),
+            pltpu.VMEM((8, KEPT, TILE), F32),
+            dma((3,)), dma((4,)), dma((4,)), dma((4, 4)), dma((4, 4)), dma((2, 4, 2)), dma((2, 4, 2)), dma((8,)), dma((8,)),
         ],
         compiler_params=pltpu.CompilerParams(
             collective_id=0, has_side_effects=True, vmem_limit_bytes=62 << 20
@@ -255,100 +290,204 @@
 
 
 def cosine_kernel(
-    block, out, paired, times, freqs, gathered, final,
-    core_send, core_recv, chip_send, chip_recv, back_send, back_recv, end_send, end_recv,
+    block, out, paired, times, times_more, freqs, freqs_more, gathered, gathered_more, final, final_more,
+    flat, mirror, mirror_half, joined,
+    swap_send, swap_recv, chip_send, chip_recv, more_send, more_recv, back_send, back_recv,
+    back_more_send, back_more_recv, end_send, end_recv, mirror_send, mirror_recv,
 ):
     row, tm = lax.axis_index("row"), lax.axis_index("tm")
     chip, core = lax.div(tm, 2), lax.rem(tm, 2)
     partner = {"row": row, "tm": chip * 2 + 1 - core}
+    has_more = lax.rem(chip, 5) == 0
 
     def other(i):
         return lax.rem(lax.div(chip, 4) + lax.div(i, 4), 4) * 4 + lax.rem(lax.rem(chip, 4) + lax.rem(i, 4), 4)
 
+    def device(target):
+        return {"row": row, "tm": target * 2 + core}
+
+    def aligned(start, size):
+        return pl.ds(pl.multiple_of(start, size), size)
+
     barrier = pltpu.get_barrier_semaphore()
 
     def greet(i, carry):
-        pl.semaphore_signal(barrier, inc=1, device_id={"row": row, "tm": other(i) * 2 + core})
+        pl.semaphore_signal(barrier, inc=1, device_id=device(other(i)))
+        return carry
+
+    def greet_row(i, carry):
+        pl.semaphore_signal(barrier, inc=1, device_id={"row": lax.rem(row + i, 8), "tm": tm})
         return carry
 
     lax.fori_loop(1, 16, greet, 0)
+    lax.fori_loop(1, 8, greet_row, 0)
     pl.semaphore_signal(barrier, inc=1, device_id=partner)
-    pl.semaphore_wait(barrier, 16)
+    pl.semaphore_wait(barrier, 23)
 
     swap = pltpu.make_async_remote_copy(
-        block.at[pl.ds(pl.multiple_of((1 - core) * 512, 512), 512)], paired.at[core],
-        core_send, core_recv, device_id=partner,
+        block.at[aligned((1 - core) * SHARE, SHARE)], paired.at[core], swap_send, swap_recv, device_id=partner,
     )
     swap.start()
-    paired[core] = block[pl.ds(pl.multiple_of(core * 512, 512), 512)]
+    paired[core] = block[aligned(core * SHARE, SHARE)]
     swap.wait()
+
+    def more_copy(e):
+        return pltpu.make_async_remote_copy(
+            paired.at[:, MAIN + e * 8:MAIN + e * 8 + 8], times_more.at[chip],
+            more_send.at[e], more_recv, device_id=device(5 * e),
+        )
 
     def spread(i, carry):
         target = other(i)
         pltpu.make_async_remote_copy(
-            paired.at[:, pl.ds(pl.multiple_of(target * 32, 32), 32)], times.at[chip],
-            chip_send, chip_recv, device_id={"row": row, "tm": target * 2 + core},
+            paired.at[:, aligned(target * 16, 16)], times.at[chip],
+            chip_send, chip_recv, device_id=device(target),
         ).start()
         return carry
 
     lax.fori_loop(1, 16, spread, 0)
-    times[chip] = paired[:, pl.ds(pl.multiple_of(chip * 32, 32), 32)]
+    for e in range(4):
+        @pl.when(chip != 5 * e)
+        def _():
+            more_copy(e).start()
+
+        @pl.when(chip == 5 * e)
+        def _():
+            times_more[chip] = paired[:, MAIN + e * 8:MAIN + e * 8 + 8]
+    times[chip] = paired[:, aligned(chip * 16, 16)]
     pltpu.make_async_copy(times.at[pl.ds(0, 15)], times.at[pl.ds(0, 15)], chip_recv).wait()
 
-    def transform(i, carry):
-        rows = pl.ds(pl.multiple_of(i * 8, 8), 8)
-        at = [times[t // 2, t % 2, rows] for t in range(32)]
+    def transform(source, result, rows):
+        at = [source[t // 2, t % 2, rows] for t in range(32)]
         mixed = ([at[t] + at[31 - t] for t in range(16)], [at[t] - at[31 - t] for t in range(16)])
         for freq in range(32):
             value = None
             for t in range(16):
                 term = cosine(freq, t) * mixed[freq % 2][t]
                 value = term if value is None else value + term
-            freqs[freq // 2, freq % 2, rows] = value
-        return carry
-
-    lax.fori_loop(0, 4, transform, 0)
+            result[freq // 2, freq % 2, rows] = value
+
+    def transform_main(i, carry):
+        transform(times, freqs, aligned(i * 8, 8))
+        return carry
+
+    lax.fori_loop(0, 2, transform_main, 0)
 
     def give(i, carry):
         target = other(i)
         pltpu.make_async_remote_copy(
-            freqs.at[target], gathered.at[chip],
-            back_send, back_recv, device_id={"row": row, "tm": target * 2 + core},
+            freqs.at[target], gathered.at[chip], back_send, back_recv, device_id=device(target),
         ).start()
         return carry
 
     lax.fori_loop(1, 16, give, 0)
+
+    def back_more_copy(target, e):
+        return pltpu.make_async_remote_copy(
+            freqs_more.at[target], gathered_more.at[e],
+            back_more_send, back_more_recv.at[e], device_id=device(target),
+        )
+
+    @pl.when(has_more)
+    def _():
+        pltpu.make_async_copy(times_more.at[pl.ds(0, 15)], times_more.at[pl.ds(0, 15)], more_recv).wait()
+        transform(times_more, freqs_more, pl.ds(0, 8))
+
+        def give_more(i, carry):
+            back_more_copy(other(i), lax.div(chip, 5)).start()
+            return carry
+
+        lax.fori_loop(1, 16, give_more, 0)
+        gathered_more[lax.div(chip, 5)] = freqs_more[chip]
+
     gathered[chip] = freqs[chip]
     pltpu.make_async_copy(gathered.at[pl.ds(0, 15)], gathered.at[pl.ds(0, 15)], back_recv).wait()
-
     last = pltpu.make_async_remote_copy(
-        gathered.at[:, 1 - core], final.at[core], end_send, end_recv, device_id=partner
+        gathered.at[:, 1 - core], final.at[core], end_send.at[0], end_recv.at[0], device_id=partner
     )
     last.start()
+    for e in range(4):
+        @pl.when(chip != 5 * e)
+        def _():
+            back_more_copy(chip, e).wait_recv()
+    last_more = pltpu.make_async_remote_copy(
+        gathered_more.at[:, 1 - core], final_more.at[core], end_send.at[1], end_recv.at[1], device_id=partner
+    )
+    last_more.start()
     final[core] = gathered[:, core]
+    final_more[core] = gathered_more[:, core]
     last.wait()
-    for j in range(8):
-        for part in range(4):
-            out[0, part * 32:(part + 1) * 32, j * TILE:(j + 1) * TILE] = final[j // 4, (j % 4) * 4 + part]
-
+    last_more.wait()
+    for c in range(2):
+        for p in range(16):
+            flat[c * SHARE + p * 16:c * SHARE + p * 16 + 16] = final[c, p]
+        for e in range(4):
+            flat[c * SHARE + MAIN + e * 8:c * SHARE + MAIN + e * 8 + 8] = final_more[c, e]
+
+    mirrors = []
+    for d in range(1, 5):
+        part, to = (pl.ds(d * TILE, TILE), mirror.at[d - 1]) if d < 4 else (pl.ds(4 * TILE, 64), mirror_half)
+        mirrors.append(pltpu.make_async_remote_copy(
+            flat.at[part], to, mirror_send.at[d - 1], mirror_recv.at[d - 1],
+            device_id={"row": lax.rem(row + d, 8), "tm": tm},
+        ))
+        mirrors[-1].start()
+
+    def columns(j):
+        return aligned(lax.rem(j, 8) * TILE, TILE)
+
+    for d in range(4):
+        out[0, :, columns(row + d)] = flat[d * TILE:(d + 1) * TILE]
+    for d in range(1, 4):
+        mirrors[d - 1].wait_recv()
+        out[0, :, columns(row + 8 - d)] = mirror[d - 1].T
+    mirrors[3].wait_recv()
+    upper = lax.div(row, 4)
+    joined[aligned(upper * 64, 64)] = flat[4 * TILE:KEPT]
+    joined[aligned((1 - upper) * 64, 64)] = mirror_half[...]
+
+    @pl.when(upper == 0)
+    def _():
+        out[0, :, columns(row + 4)] = joined[...]
+
+    @pl.when(upper == 1)
+    def _():
+        out[0, :, columns(row + 4)] = joined[...].T
+
+    for copy in mirrors:
+        copy.wait_send()
     pltpu.make_async_copy(times.at[pl.ds(0, 15)], times.at[pl.ds(0, 15)], chip_send).wait()
     pltpu.make_async_copy(times.at[pl.ds(0, 15)], times.at[pl.ds(0, 15)], back_send).wait()
+    for e in range(4):
+        @pl.when(chip != 5 * e)
+        def _():
+            more_copy(e).wait_send()
+
+    @pl.when(has_more)
+    def _():
+        pltpu.make_async_copy(times_more.at[pl.ds(0, 15)], times_more.at[pl.ds(0, 15)], back_more_send).wait()
 
 
 def cosine_sums(block):
     dma = pltpu.SemaphoreType.DMA
+    main = pltpu.VMEM((16, 2, 16, TILE), F32)
+    more = pltpu.VMEM((16, 2, 8, TILE), F32)
     return pl.pallas_call(
         cosine_kernel,
         out_shape=jax.ShapeDtypeStruct((1, TILE, 1024), F32),
         in_specs=[pl.BlockSpec(memory_space=pltpu.VMEM)],
         out_specs=pl.BlockSpec(memory_space=pltpu.VMEM),
         scratch_shapes=[
-            pltpu.VMEM((2, 512, TILE), F32),
-            pltpu.VMEM((16, 2, 32, TILE), F32),
-            pltpu.VMEM((16, 2, 32, TILE), F32),
-            pltpu.VMEM((16, 2, 32, TILE), F32),
-            pltpu.VMEM((2, 16, 32, TILE), F32),
-            dma, dma, dma, dma, dma, dma, dma, dma,
+            pltpu.VMEM((2, SHARE, TILE), F32),
+            main, more, main, more, main,
+            pltpu.VMEM((4, 2, 8, TILE), F32),
+            pltpu.VMEM((2, 16, 16, TILE), F32),
+            pltpu.VMEM((2, 4, 8, TILE), F32),
+            pltpu.VMEM((KEPT, TILE), F32),
+            pltpu.VMEM((3, TILE, TILE), F32),
+            pltpu.VMEM((64, TILE), F32),
+            pltpu.VMEM((TILE, TILE), F32),
+            dma, dma, dma, dma, dma((4,)), dma, dma, dma, dma, dma((4,)), dma((2,)), dma((2,)), dma((4,)), dma((4,)),
         ],
         compiler_params=pltpu.CompilerParams(
             collective_id=1, has_side_effects=True, vmem_limit_bytes=16 << 20

time: 226 us -> 198 us (0.88)
  Pallas kernels: 224 us -> 196 us
    pallas_call x1, Pallas kernels: 181 us -> 157 us  [green_sums(): pl.pallas_call(green_kernel, out_shape=jax.ShapeDtypeStruct((KEPT, TILE),...]
    pallas_call x1, Pallas kernels: 42.7 us -> 39.3 us  [cosine_sums(): pl.pallas_call(cosine_kernel, out_shape=jax.ShapeDtypeStruct((1, TILE, 10...]
where the time goes in v2:
time: 198 us
  Pallas kernels  196 us (99%)
    pallas_call x1, Pallas kernels, green_sums(): pl.pallas_call(green_kernel, out_shape=jax.ShapeDtypeStruct((KEPT, TILE),...  157 us
    pallas_call x1, Pallas kernels, cosine_sums(): pl.pallas_call(cosine_kernel, out_shape=jax.ShapeDtypeStruct((1, TILE, 10...  39.3 us

profile of v2, /device:TPU:1, one launch (start us, length us, event | category | flops | bytes accessed | tf_op | source)
XLA Modules:
  0.0 197.8 jit_solution(3471942899910453513)
XLA Ops:
  0.0 156.8 %green_sums.1.block = f32[576,128]{1,0:T(8,128)} custom-call(f32[1,256,2048]{2,1,0:T(8,128)} %occ.1, f32[1,256,2048]{2,1,0:T(8,128)} %vir.1, f32[256,1024]{1,0:T(8,128)} %eps.1), custom_call_target="tpu_custom_call" | custom-call | flops 20000000000 | bytes 20971520 | tf_op jit(solution)/shard_map/green_sums/pallas_call | solution.py:260
  156.8 0.0 copy-start
  156.8 1.0 copy-done
  157.7 39.3 %cosine_sums.1 = f32[1,128,1024]{2,1,0:T(8,128)S(1)} custom-call(f32[576,128]{1,0:T(8,128)S(1)} %copy-done), custom_call_target="tpu_custom_call" | custom-call | flops 10000000 | bytes 1048576 | tf_op jit(solution)/shard_map/cosine_sums/pallas_call | solution.py:475
  197.0 0.8 copy.5
Async XLA Ops:
  156.8 1.0 copy-start

commit v3 on v2

--- a/solution.py
+++ b/solution.py
@@ -15,12 +15,24 @@
 TN_DIMS = (((0,), (0,)), ((), ()))
 NEXT, OWN, ACROSS, FAR = 0, 1, 2, 3
 ROWS = 256
-HALF = 128
+PARTS = ((0, 128), (128, 128))
 TILE = 128
 QUARTER = 64
 KEPT = 4 * TILE + 64
 SHARE = KEPT // 2
 MAIN = 256
+GREEN_SCRATCH = 20
+
+
+def ring_place(row):
+    y, z = lax.div(row, 2), lax.rem(row, 2)
+    return y + z * (7 - 2 * y)
+
+
+def ring_row(place):
+    place = lax.rem(place, 8)
+    z = lax.div(place, 4)
+    return (place + z * (7 - 2 * place)) * 2 + z
 
 
 def halves_of(x):
@@ -45,21 +57,10 @@
     x = lax.div(tm, 8)
     beside = [{"row": row, "tm": lax.rem(tm + 8 * i, 32)} for i in range(4)]
 
-    barrier = pltpu.get_barrier_semaphore()
-
-    def greet(i, carry):
-        pl.semaphore_signal(barrier, inc=1, device_id={"row": lax.rem(row + i, 8), "tm": tm})
-        return carry
-
-    lax.fori_loop(1, 8, greet, 0)
-    for i in range(1, 4):
-        pl.semaphore_signal(barrier, inc=1, device_id=beside[i])
-    pl.semaphore_wait(barrier, 10)
-
     def block(slot, chunk=None):
         if chunk is None:
             return pl.ds(slot * ROWS, ROWS)
-        return pl.ds(slot * ROWS + chunk * HALF, HALF)
+        return pl.ds(slot * ROWS + PARTS[chunk][0], PARTS[chunk][1])
 
     def quarter(slot, of):
         return pl.ds(pl.multiple_of(slot * ROWS + of * QUARTER, QUARTER), QUARTER)
@@ -93,9 +94,9 @@
     copies = {}
     copies["basis", NEXT] = send_basis(eps.at[quarter(0, x)], NEXT, before)
     copies["basis", ACROSS] = send_basis(eps.at[quarter(0, x)], ACROSS, across)
-    for chunk in range(2):
+    for chunk in range(len(PARTS)):
         for which in range(2):
-            part = sources[which].at[pl.ds(chunk * HALF, HALF)]
+            part = sources[which].at[pl.ds(*PARTS[chunk])]
             copies[which, NEXT, chunk] = send_rows(which, chunk, part, NEXT, before)
             copies[which, ACROSS, chunk] = send_rows(which, chunk, part, ACROSS, across)
     for copy in copies.values():
@@ -108,8 +109,8 @@
     for copy in own:
         copy.wait()
 
-    def convert(slot, chunk):
-        start = slot * ROWS + chunk * HALF
+    def convert(slot, first, size):
+        start = slot * ROWS + first
 
         def body(i, carry):
             rows = pl.ds(start + i * 16, 16)
@@ -117,7 +118,7 @@
                 high[which, rows], low[which, rows] = halves_of(full[which, rows])
             return carry
 
-        lax.fori_loop(0, HALF // 16, body, 0)
+        lax.fori_loop(0, size // 16, body, 0)
 
     def convert_basis(slot):
         def body(i, carry):
@@ -127,91 +128,92 @@
 
         lax.fori_loop(0, ROWS // 16, body, 0)
 
-    def greens(left, right, width, weight):
+    def greens(left, size, right, width, weight):
         def one(which):
-            lhs = (high[which, pl.ds(left, HALF)], low[which, pl.ds(left, HALF)])
+            lhs = (high[which, pl.ds(left, size)], low[which, pl.ds(left, size)])
             rhs = (high[which, pl.ds(right, width)], low[which, pl.ds(right, width)])
             return dot3(lhs, rhs, NT_DIMS)
 
-        polar[:, pl.ds(right, width)] = weight * (one(0) * one(1))
-
-    def project(left, spans, first):
+        polar[0:size, pl.ds(right, width)] = weight * (one(0) * one(1))
+
+    def project(left, size, spans, first):
         term = None
         for start, width in spans:
             rhs = (basis_high[pl.ds(start, width)], basis_low[pl.ds(start, width)])
-            new = dot3(halves_of(polar[:, pl.ds(start, width)]), rhs, NN_DIMS)
+            new = dot3(halves_of(polar[0:size, pl.ds(start, width)]), rhs, NN_DIMS)
             term = new if term is None else term + new
         term = halves_of(term)
 
         def body(i, carry):
             columns = pl.ds(pl.multiple_of(i * 256, 256), 256)
-            lhs = (basis_high[pl.ds(left, HALF), columns], basis_low[pl.ds(left, HALF), columns])
+            lhs = (basis_high[pl.ds(left, size), columns], basis_low[pl.ds(left, size), columns])
             new = dot3(lhs, term, TN_DIMS)
             total[columns] = new if first else total[columns] + new
             return carry
 
         lax.fori_loop(0, 4, body, 0)
 
-    def at(slot, chunk=0):
-        return slot * ROWS + chunk * HALF
+    def at(slot, first=0):
+        return slot * ROWS + first
 
     def wait_rows(slot, chunk):
         for which in range(2):
             copies[which, slot, chunk].wait_recv()
 
-    def work(slot, chunk, spans, first=False):
+    def work(slot, first, size, spans, opening=False):
         for start, width, weight in spans:
-            greens(at(slot, chunk), start, width, weight)
-        project(at(slot, chunk), [span[:2] for span in spans], first)
+            greens(at(slot, first), size, start, width, weight)
+        project(at(slot, first), size, [span[:2] for span in spans], opening)
 
     convert_basis(OWN)
     share_basis(NEXT)
     copies["basis", FAR] = send_basis(basis.at[quarter(NEXT, x)], FAR, before)
     copies["basis", FAR].start()
     share_basis(ACROSS)
-    for chunk in range(2):
-        convert(OWN, chunk)
-    work(OWN, 0, [(at(OWN), ROWS, 0.5)], first=True)
-    work(OWN, 1, [(at(OWN), ROWS, 0.5)])
-    share_basis(FAR)
-    take_basis(NEXT)
-    take_basis(ACROSS)
-    take_basis(FAR)
-
-    for chunk in range(2):
+    convert(OWN, 0, ROWS)
+    work(OWN, 0, 128, [(at(OWN), ROWS, 0.5)], opening=True)
+    work(OWN, 128, 128, [(at(OWN), ROWS, 0.5)])
+    for chunk in range(len(PARTS)):
         wait_rows(NEXT, chunk)
         for which in range(2):
             copies[which, FAR, chunk] = send_rows(which, chunk, full.at[which, block(NEXT, chunk)], FAR, before)
             copies[which, FAR, chunk].start()
-        convert(NEXT, chunk)
-        work(NEXT, chunk, [(at(OWN), ROWS, 1.0)])
-
-    wait_rows(ACROSS, 0)
-    convert(ACROSS, 0)
-    work(ACROSS, 0, [(at(NEXT), ROWS, 1.0), (at(OWN), ROWS, 0.5)])
-    wait_rows(FAR, 0)
-    convert(FAR, 0)
-    work(FAR, 0, [(at(OWN), ROWS, 0.5), (at(ACROSS), HALF, 0.5)])
-    wait_rows(ACROSS, 1)
-    convert(ACROSS, 1)
-    work(ACROSS, 1, [(at(NEXT), ROWS, 1.0), (at(OWN), ROWS, 0.5), (at(FAR), HALF, 0.5)])
-    wait_rows(FAR, 1)
-    convert(FAR, 1)
-    work(FAR, 1, [(at(OWN), ROWS, 0.5), (at(ACROSS), ROWS, 0.5)])
+    share_basis(FAR)
+    take_basis(NEXT)
+    convert(NEXT, 0, ROWS)
+    work(NEXT, 0, 128, [(at(OWN), ROWS, 1.0)])
+    work(NEXT, 128, 128, [(at(OWN), ROWS, 1.0)])
+
+    take_basis(ACROSS)
+    have = {ACROSS: 0, FAR: 0}
+    for chunk in range(len(PARTS)):
+        for slot, spans, mate in (
+            (ACROSS, [(at(NEXT), ROWS, 1.0), (at(OWN), ROWS, 0.5)], FAR),
+            (FAR, [(at(OWN), ROWS, 0.5)], ACROSS),
+        ):
+            if slot == FAR and chunk == 0:
+                take_basis(FAR)
+            wait_rows(slot, chunk)
+            convert(slot, *PARTS[chunk])
+            more = [(at(mate), have[mate], 0.5)] if have[mate] else []
+            work(slot, *PARTS[chunk], spans + more)
+            have[slot] += PARTS[chunk][1]
 
     def fold(owner, slot):
         def span(j):
             return pl.ds(pl.multiple_of(j * TILE, TILE), TILE)
 
         rows = span(owner)
+        place = ring_place(owner)
         for d in range(4):
-            tile = span(lax.rem(owner + d, 8))
+            tile = span(ring_row(place + d))
             staged[slot, d * TILE:(d + 1) * TILE] = total[rows, tile] + total[tile, rows].T
-        low_tile, upper = lax.rem(owner, 4), lax.div(owner, 4)
-        turned[...] = total[span(low_tile + 4), span(low_tile)].T
+        upper = lax.div(place, 4)
+        low_tile, high_tile = ring_row(lax.rem(place, 4)), ring_row(lax.rem(place, 4) + 4)
+        turned[...] = total[span(high_tile), span(low_tile)].T
         half = pl.ds(pl.multiple_of(low_tile * TILE + upper * 64, 64), 64)
         staged[slot, 4 * TILE:KEPT] = (
-            total[half, span(low_tile + 4)] + turned[pl.ds(pl.multiple_of(upper * 64, 64), 64)]
+            total[half, span(high_tile)] + turned[pl.ds(pl.multiple_of(upper * 64, 64), 64)]
         )
 
     def part_copy(owner, i):
@@ -245,43 +247,36 @@
 
     lax.fori_loop(0, KEPT // 64, add, 0)
 
-    for copy in copies.values():
-        copy.wait_send()
-
-    def drain(i, carry):
-        part_copy(row, i).wait_send()
-        return carry
-
-    lax.fori_loop(1, 8, drain, 0)
-
-
-def green_sums(occ, vir, eps):
-    dma = pltpu.SemaphoreType.DMA
-    return pl.pallas_call(
-        green_kernel,
-        out_shape=jax.ShapeDtypeStruct((KEPT, TILE), F32),
-        in_specs=[pl.BlockSpec(memory_space=pl.ANY)] * 3,
-        out_specs=pl.BlockSpec(memory_space=pltpu.VMEM),
-        scratch_shapes=[
-            pltpu.VMEM((2, 4 * ROWS, 2048), F32),
-            pltpu.VMEM((2, 4 * ROWS, 2048), BF16),
-            pltpu.VMEM((2, 4 * ROWS, 2048), BF16),
-            pltpu.VMEM((4 * ROWS, 1024), F32),
-            pltpu.VMEM((4 * ROWS, 1024), BF16),
-            pltpu.VMEM((4 * ROWS, 1024), BF16),
-            pltpu.VMEM((HALF, 4 * ROWS), F32),
-            pltpu.VMEM((1024, 1024), F32),
-            pltpu.VMEM((TILE, TILE), F32),
-            pltpu.VMEM((8, KEPT, TILE), F32),
-            pltpu.VMEM((8, KEPT, TILE), F32),
-            dma((3,)), dma((4,)), dma((4,)), dma((4, 4)), dma((4, 4)), dma((2, 4, 2)), dma((2, 4, 2)), dma((8,)), dma((8,)),
-        ],
-        compiler_params=pltpu.CompilerParams(
-            collective_id=0, has_side_effects=True, vmem_limit_bytes=62 << 20
-        ),
-        cost_estimate=pl.CostEstimate(flops=20 * 10**9, bytes_accessed=20 << 20, transcendentals=0),
-        name="green_sums",
-    )(occ, vir, eps)
+    def finish():
+        for copy in copies.values():
+            copy.wait_send()
+
+        def drain(i, carry):
+            part_copy(row, i).wait_send()
+            return carry
+
+        lax.fori_loop(1, 8, drain, 0)
+
+    return finish
+
+
+def meet():
+    row, tm = lax.axis_index("row"), lax.axis_index("tm")
+    chip, core = lax.div(tm, 2), lax.rem(tm, 2)
+    barrier = pltpu.get_barrier_semaphore()
+
+    def greet_row(i, carry):
+        pl.semaphore_signal(barrier, inc=1, device_id={"row": lax.rem(row + i, 8), "tm": tm})
+        return carry
+
+    def greet_chip(i, carry):
+        pl.semaphore_signal(barrier, inc=1, device_id={"row": row, "tm": lax.rem(chip + i, 16) * 2 + core})
+        return carry
+
+    lax.fori_loop(1, 8, greet_row, 0)
+    lax.fori_loop(1, 16, greet_chip, 0)
+    pl.semaphore_signal(barrier, inc=1, device_id={"row": row, "tm": chip * 2 + 1 - core})
+    pl.semaphore_wait(barrier, 23)
 
 
 def cosine(freq, time):
@@ -308,21 +303,6 @@
 
     def aligned(start, size):
         return pl.ds(pl.multiple_of(start, size), size)
-
-    barrier = pltpu.get_barrier_semaphore()
-
-    def greet(i, carry):
-        pl.semaphore_signal(barrier, inc=1, device_id=device(other(i)))
-        return carry
-
-    def greet_row(i, carry):
-        pl.semaphore_signal(barrier, inc=1, device_id={"row": lax.rem(row + i, 8), "tm": tm})
-        return carry
-
-    lax.fori_loop(1, 16, greet, 0)
-    lax.fori_loop(1, 8, greet_row, 0)
-    pl.semaphore_signal(barrier, inc=1, device_id=partner)
-    pl.semaphore_wait(barrier, 23)
 
     swap = pltpu.make_async_remote_copy(
         block.at[aligned((1 - core) * SHARE, SHARE)], paired.at[core], swap_send, swap_recv, device_id=partner,
@@ -425,34 +405,35 @@
             flat[c * SHARE + MAIN + e * 8:c * SHARE + MAIN + e * 8 + 8] = final_more[c, e]
 
     mirrors = []
+    place = ring_place(row)
     for d in range(1, 5):
         part, to = (pl.ds(d * TILE, TILE), mirror.at[d - 1]) if d < 4 else (pl.ds(4 * TILE, 64), mirror_half)
         mirrors.append(pltpu.make_async_remote_copy(
             flat.at[part], to, mirror_send.at[d - 1], mirror_recv.at[d - 1],
-            device_id={"row": lax.rem(row + d, 8), "tm": tm},
+            device_id={"row": ring_row(place + d), "tm": tm},
         ))
         mirrors[-1].start()
 
     def columns(j):
-        return aligned(lax.rem(j, 8) * TILE, TILE)
+        return aligned(ring_row(j) * TILE, TILE)
 
     for d in range(4):
-        out[0, :, columns(row + d)] = flat[d * TILE:(d + 1) * TILE]
+        out[0, :, columns(place + d)] = flat[d * TILE:(d + 1) * TILE]
     for d in range(1, 4):
         mirrors[d - 1].wait_recv()
-        out[0, :, columns(row + 8 - d)] = mirror[d - 1].T
+        out[0, :, columns(place + 8 - d)] = mirror[d - 1].T
     mirrors[3].wait_recv()
-    upper = lax.div(row, 4)
+    upper = lax.div(place, 4)
     joined[aligned(upper * 64, 64)] = flat[4 * TILE:KEPT]
     joined[aligned((1 - upper) * 64, 64)] = mirror_half[...]
 
     @pl.when(upper == 0)
     def _():
-        out[0, :, columns(row + 4)] = joined[...]
+        out[0, :, columns(place + 4)] = joined[...]
 
     @pl.when(upper == 1)
     def _():
-        out[0, :, columns(row + 4)] = joined[...].T
+        out[0, :, columns(place + 4)] = joined[...].T
 
     for copy in mirrors:
         copy.wait_send()
@@ -468,16 +449,41 @@
         pltpu.make_async_copy(times_more.at[pl.ds(0, 15)], times_more.at[pl.ds(0, 15)], back_more_send).wait()
 
 
-def cosine_sums(block):
+def kernel(occ, vir, eps, out, block, *scratch):
+    meet()
+    finish = green_kernel(occ, vir, eps, block, *scratch[:GREEN_SCRATCH])
+    cosine_kernel(block, out, *scratch[GREEN_SCRATCH:])
+    finish()
+
+
+def on_device(occ_factor, vir_factor, eps_basis):
     dma = pltpu.SemaphoreType.DMA
     main = pltpu.VMEM((16, 2, 16, TILE), F32)
     more = pltpu.VMEM((16, 2, 8, TILE), F32)
+    rows_sems = dma((2, 4, len(PARTS)))
+    green = [
+        pltpu.VMEM((2, 4 * ROWS, 2048), F32),
+        pltpu.VMEM((2, 4 * ROWS, 2048), BF16),
+        pltpu.VMEM((2, 4 * ROWS, 2048), BF16),
+        pltpu.VMEM((4 * ROWS, 1024), F32),
+        pltpu.VMEM((4 * ROWS, 1024), BF16),
+        pltpu.VMEM((4 * ROWS, 1024), BF16),
+        pltpu.VMEM((128, 4 * ROWS), F32),
+        pltpu.VMEM((1024, 1024), F32),
+        pltpu.VMEM((TILE, TILE), F32),
+        pltpu.VMEM((8, KEPT, TILE), F32),
+        pltpu.VMEM((8, KEPT, TILE), F32),
+        dma((3,)), dma((4,)), dma((4,)), dma((4, 4)), dma((4, 4)), rows_sems, rows_sems, dma((8,)), dma((8,)),
+    ]
+    assert len(green) == GREEN_SCRATCH
     return pl.pallas_call(
-        cosine_kernel,
+        kernel,
         out_shape=jax.ShapeDtypeStruct((1, TILE, 1024), F32),
-        in_specs=[pl.BlockSpec(memory_space=pltpu.VMEM)],
+        in_specs=[pl.BlockSpec(memory_space=pl.ANY)] * 3,
         out_specs=pl.BlockSpec(memory_space=pltpu.VMEM),
         scratch_shapes=[
+            pltpu.VMEM((KEPT, TILE), F32),
+            *green,
             pltpu.VMEM((2, SHARE, TILE), F32),
             main, more, main, more, main,
             pltpu.VMEM((4, 2, 8, TILE), F32),
@@ -490,15 +496,11 @@
             dma, dma, dma, dma, dma((4,)), dma, dma, dma, dma, dma((4,)), dma((2,)), dma((2,)), dma((4,)), dma((4,)),
         ],
         compiler_params=pltpu.CompilerParams(
-            collective_id=1, has_side_effects=True, vmem_limit_bytes=16 << 20
+            collective_id=0, has_side_effects=True, vmem_limit_bytes=62 << 20
         ),
-        cost_estimate=pl.CostEstimate(flops=10**7, bytes_accessed=1 << 20, transcendentals=0),
-        name="cosine_sums",
-    )(block)
-
-
-def on_device(occ_factor, vir_factor, eps_basis):
-    return cosine_sums(green_sums(occ_factor, vir_factor, eps_basis))
+        cost_estimate=pl.CostEstimate(flops=20 * 10**9, bytes_accessed=20 << 20, transcendentals=0),
+        name="polarizability",
+    )(occ_factor, vir_factor, eps_basis)
 
 
 def solution(mesh):

time: 198 us -> 186 us (0.939)
  Pallas kernels: 196 us -> 183 us
    pallas_call x2 -> x1, Pallas kernels: 196 us -> 183 us  [on_device(): pl.pallas_call(kernel, out_shape=jax.ShapeDtypeStruct((1, TILE, 1024), F3...]
where the time goes in v3:
time: 186 us; the launch traced here: 185 us
  Pallas kernels  183 us (98%)
  local copies, waits for them, and re-layouts  1.89 us (1%)
    pallas_call x1, Pallas kernels, on_device(): pl.pallas_call(kernel, out_shape=jax.ShapeDtypeStruct((1, TILE, 1024), F3...  183 us

profile of v3, /device:TPU:1, one launch (start us, length us, event | category | flops | bytes accessed | tf_op | source)
XLA Modules:
  0.0 184.8 jit_solution(1271108531545094036)
XLA Ops:
  0.0 182.9 %polarizability.1 = f32[1,128,1024]{2,1,0:T(8,128)} custom-call(f32[1,256,2048]{2,1,0:T(8,128)} %occ.1, f32[1,256,2048]{2,1,0:T(8,128)} %vir.1, f32[256,1024]{1,0:T(8,128)} %eps.1), custom_call_target="tpu_custom_call" | custom-call | flops 20000000000 | bytes 20971520 | tf_op jit(solution)/shard_map/polarizability/pallas_call | solution.py:479
  182.9 1.9 %copy.5 = f32[1,128,1024]{2,1,0:T(8,128)} copy(f32[1,128,1024]{2,1,0:T(8,128)} %polarizability.1) | data formatting | bytes 1048576

commit v4 on v3

--- a/solution.py
+++ b/solution.py
@@ -13,15 +13,17 @@
 NT_DIMS = (((1,), (1,)), ((), ()))
 NN_DIMS = (((1,), (0,)), ((), ()))
 TN_DIMS = (((0,), (0,)), ((), ()))
-NEXT, OWN, ACROSS, FAR = 0, 1, 2, 3
+OWN, NEXT, ACROSS, FAR = 0, 1, 2, 3
 ROWS = 256
-PARTS = ((0, 128), (128, 128))
+EARLY, LATE = 192, 64
+PARTS = ((0, EARLY), (EARLY, LATE))
+MEETING = (EARLY, LATE + 2 * ROWS)
 TILE = 128
 QUARTER = 64
 KEPT = 4 * TILE + 64
 SHARE = KEPT // 2
 MAIN = 256
-GREEN_SCRATCH = 20
+GREEN_SCRATCH = 22
 
 
 def ring_place(row):
@@ -46,7 +48,7 @@
 
 
 def green_kernel(
-    occ, vir, eps, out, full, high, low, basis, basis_high, basis_low, polar, total, turned, staged, arrived,
+    occ, vir, eps, out, full, high, low, basis, basis_high, basis_low, polar, late, late_basis, total, turned, staged, arrived,
     local_sem, basis_send, basis_recv, share_send, share_recv, send, recv, part_send, part_recv,
 ):
     row, tm = lax.axis_index("row"), lax.axis_index("tm")
@@ -149,6 +151,61 @@
             lhs = (basis_high[pl.ds(left, size), columns], basis_low[pl.ds(left, size), columns])
             new = dot3(lhs, term, TN_DIMS)
             total[columns] = new if first else total[columns] + new
+            return carry
+
+        lax.fori_loop(0, 4, body, 0)
+
+    def convert_late(k, slot):
+        def body(i, carry):
+            rows = pl.ds(slot * ROWS + EARLY + i * 16, 16)
+            for which in range(2):
+                upper, lower = halves_of(full[which, rows])
+                late[which, pl.ds(k * LATE + i * 16, 16)] = upper
+                late[which, pl.ds((2 + k) * LATE + i * 16, 16)] = lower
+                if slot == ACROSS:
+                    high[which, rows], low[which, rows] = upper, lower
+            return carry
+
+        lax.fori_loop(0, LATE // 16, body, 0)
+
+    def prepare_late_basis():
+        for k, slot in enumerate((ACROSS, FAR)):
+            rows = basis[slot * ROWS + EARLY:(slot + 1) * ROWS]
+            turned[k * LATE:(k + 1) * LATE, :] = rows
+        upper, lower = halves_of(turned[0:TILE].T)
+        late_basis[:, 0:TILE] = upper
+        late_basis[:, TILE:2 * TILE] = upper
+        late_basis[:, 2 * TILE:3 * TILE] = lower
+
+    def late_work():
+        rows = pl.ds(*MEETING)
+
+        def one(which):
+            both = lax.dot_general(high[which, rows], late[which], NT_DIMS, preferred_element_type=F32)
+            rest = lax.dot_general(low[which, rows], late[which, 0:TILE], NT_DIMS, preferred_element_type=F32)
+            return both[:, 0:TILE] + (both[:, TILE:] + rest)
+
+        at_row = lax.broadcasted_iota(jnp.int32, (MEETING[1], TILE), 0)
+        across_side = lax.broadcasted_iota(jnp.int32, (MEETING[1], TILE), 1) < LATE
+        weight = jnp.where(
+            at_row < LATE, 0.5,
+            jnp.where(
+                at_row < LATE + ROWS, jnp.where(across_side, 1.0, 0.0),
+                jnp.where(across_side, 0.0, jnp.where(at_row < LATE + ROWS + EARLY, 1.0, 0.5)),
+            ),
+        )
+        upper, lower = halves_of((weight * (one(0) * one(1))).T)
+        both = jnp.concatenate([upper, lower], axis=0)
+        term = lax.dot_general(both, basis_high[rows], NN_DIMS, preferred_element_type=F32)
+        term = term[0:TILE] + (
+            term[TILE:] + lax.dot_general(upper, basis_low[rows], NN_DIMS, preferred_element_type=F32)
+        )
+        upper, lower = halves_of(term)
+        rhs = jnp.concatenate([upper, lower, upper], axis=0)
+
+        def body(i, carry):
+            part = pl.ds(pl.multiple_of(i * 256, 256), 256)
+            total[part] += lax.dot_general(late_basis[part], rhs, NN_DIMS, preferred_element_type=F32)
             return carry
 
         lax.fori_loop(0, 4, body, 0)
@@ -185,19 +242,20 @@
     work(NEXT, 128, 128, [(at(OWN), ROWS, 1.0)])
 
     take_basis(ACROSS)
-    have = {ACROSS: 0, FAR: 0}
-    for chunk in range(len(PARTS)):
-        for slot, spans, mate in (
-            (ACROSS, [(at(NEXT), ROWS, 1.0), (at(OWN), ROWS, 0.5)], FAR),
-            (FAR, [(at(OWN), ROWS, 0.5)], ACROSS),
-        ):
-            if slot == FAR and chunk == 0:
-                take_basis(FAR)
-            wait_rows(slot, chunk)
-            convert(slot, *PARTS[chunk])
-            more = [(at(mate), have[mate], 0.5)] if have[mate] else []
-            work(slot, *PARTS[chunk], spans + more)
-            have[slot] += PARTS[chunk][1]
+    take_basis(FAR)
+    prepare_late_basis()
+    own_weight = jnp.where(lax.broadcasted_iota(jnp.int32, (1, 2 * ROWS), 1) < EARLY, 0.5, 1.0)
+    wait_rows(ACROSS, 0)
+    convert(ACROSS, 0, EARLY)
+    work(ACROSS, 0, EARLY, [(at(OWN), 2 * ROWS, own_weight)])
+    wait_rows(FAR, 0)
+    convert(FAR, 0, EARLY)
+    work(FAR, 0, EARLY, [(at(OWN), ROWS, own_weight[:, 0:ROWS]), (at(ACROSS), EARLY, 0.5)])
+    wait_rows(ACROSS, 1)
+    convert_late(0, ACROSS)
+    wait_rows(FAR, 1)
+    convert_late(1, FAR)
+    late_work()
 
     def fold(owner, slot):
         def span(j):
@@ -210,10 +268,10 @@
             staged[slot, d * TILE:(d + 1) * TILE] = total[rows, tile] + total[tile, rows].T
         upper = lax.div(place, 4)
         low_tile, high_tile = ring_row(lax.rem(place, 4)), ring_row(lax.rem(place, 4) + 4)
-        turned[...] = total[span(high_tile), span(low_tile)].T
+        turned[:, 0:TILE] = total[span(high_tile), span(low_tile)].T
         half = pl.ds(pl.multiple_of(low_tile * TILE + upper * 64, 64), 64)
         staged[slot, 4 * TILE:KEPT] = (
-            total[half, span(high_tile)] + turned[pl.ds(pl.multiple_of(upper * 64, 64), 64)]
+            total[half, span(high_tile)] + turned[pl.ds(pl.multiple_of(upper * 64, 64), 64), 0:TILE]
         )
 
     def part_copy(owner, i):
@@ -468,9 +526,11 @@
         pltpu.VMEM((4 * ROWS, 1024), F32),
         pltpu.VMEM((4 * ROWS, 1024), BF16),
         pltpu.VMEM((4 * ROWS, 1024), BF16),
-        pltpu.VMEM((128, 4 * ROWS), F32),
+        pltpu.VMEM((EARLY, 4 * ROWS), F32),
+        pltpu.VMEM((2, 4 * LATE, 2048), BF16),
+        pltpu.VMEM((1024, 3 * TILE), BF16),
         pltpu.VMEM((1024, 1024), F32),
-        pltpu.VMEM((TILE, TILE), F32),
+        pltpu.VMEM((TILE, 1024), F32),
         pltpu.VMEM((8, KEPT, TILE), F32),
         pltpu.VMEM((8, KEPT, TILE), F32),
         dma((3,)), dma((4,)), dma((4,)), dma((4, 4)), dma((4, 4)), rows_sems, rows_sems, dma((8,)), dma((8,)),

time: 186 us -> 177 us (0.952)
  Pallas kernels: 183 us -> 174 us
    pallas_call x1, Pallas kernels: 183 us -> 174 us  [on_device(): pl.pallas_call(kernel, out_shape=jax.ShapeDtypeStruct((1, TILE, 1024), F3...]
where the time goes in v4:
time: 177 us; the launch traced here: 176 us
  Pallas kernels  174 us (98%)
  local copies, waits for them, and re-layouts  1.89 us (1%)
    pallas_call x1, Pallas kernels, on_device(): pl.pallas_call(kernel, out_shape=jax.ShapeDtypeStruct((1, TILE, 1024), F3...  174 us

profile of v4, /device:TPU:1, one launch (start us, length us, event | category | flops | bytes accessed | tf_op | source)
XLA Modules:
  0.0 176.0 jit_solution(16264553807285023089)
XLA Ops:
  0.0 174.1 %polarizability.1 = f32[1,128,1024]{2,1,0:T(8,128)} custom-call(f32[1,256,2048]{2,1,0:T(8,128)} %occ.1, f32[1,256,2048]{2,1,0:T(8,128)} %vir.1, f32[256,1024]{1,0:T(8,128)} %eps.1), custom_call_target="tpu_custom_call" | custom-call | flops 20000000000 | bytes 20971520 | tf_op jit(solution)/shard_map/polarizability/pallas_call | solution.py:539
  174.1 1.9 %copy.5 = f32[1,128,1024]{2,1,0:T(8,128)} copy(f32[1,128,1024]{2,1,0:T(8,128)} %polarizability.1) | data formatting | bytes 1048576

commit v5 on v4

--- a/solution.py
+++ b/solution.py
@@ -48,7 +48,7 @@
 
 
 def green_kernel(
-    occ, vir, eps, out, full, high, low, basis, basis_high, basis_low, polar, late, late_basis, total, turned, staged, arrived,
+    occ, vir, eps, full, high, low, basis, basis_high, basis_low, polar, late, late_basis, total, turned, staged, arrived,
     local_sem, basis_send, basis_recv, share_send, share_recv, send, recv, part_send, part_recv,
 ):
     row, tm = lax.axis_index("row"), lax.axis_index("tm")
@@ -274,48 +274,60 @@
             total[half, span(high_tile)] + turned[pl.ds(pl.multiple_of(upper * 64, 64), 64), 0:TILE]
         )
 
-    def part_copy(owner, i):
+    core = lax.rem(tm, 2)
+
+    def half_rows(half):
+        return pl.ds(pl.multiple_of(half * SHARE, SHARE), SHARE)
+
+    def part_copy(owner, i, half):
         return pltpu.make_async_remote_copy(
-            staged.at[i], arrived.at[i], part_send.at[i], part_recv.at[i],
+            staged.at[i, half_rows(half)], arrived.at[i, half_rows(half)], part_send.at[half, i], part_recv.at[half, i],
             device_id={"row": owner, "tm": tm},
         )
 
-    def send_part(i, carry):
+    def send_first(i, carry):
         owner = lax.rem(row + i, 8)
         fold(owner, i)
-        part_copy(owner, i).start()
+        part_copy(owner, i, 1 - core).start()
         return carry
 
-    lax.fori_loop(1, 8, send_part, 0)
+    def send_second(i, carry):
+        part_copy(lax.rem(row + i, 8), i, core).start()
+        return carry
+
+    lax.fori_loop(1, 8, send_first, 0)
+    lax.fori_loop(1, 8, send_second, 0)
     fold(row, 0)
 
-    def take_part(i, carry):
-        part_copy(row, i).wait_recv()
-        return carry
-
-    lax.fori_loop(1, 8, take_part, 0)
-
-    def add(i, carry):
-        rows = pl.ds(i * 64, 64)
-        value = staged[0, rows]
-        for j in range(1, 8):
-            value = value + arrived[j, rows]
-        out[rows] = value
-        return carry
-
-    lax.fori_loop(0, KEPT // 64, add, 0)
+    def reduce_half(half, result):
+        def take_part(i, carry):
+            part_copy(row, i, half).wait_recv()
+            return carry
+
+        lax.fori_loop(1, 8, take_part, 0)
+
+        def add(i, carry):
+            rows = pl.ds(pl.multiple_of(half * SHARE + i * 32, 32), 32)
+            value = staged[0, rows]
+            for j in range(1, 8):
+                value = value + arrived[j, rows]
+            result[pl.ds(pl.multiple_of(i * 32, 32), 32)] = value
+            return carry
+
+        lax.fori_loop(0, SHARE // 32, add, 0)
 
     def finish():
         for copy in copies.values():
             copy.wait_send()
 
         def drain(i, carry):
-            part_copy(row, i).wait_send()
+            for half in range(2):
+                part_copy(row, i, half).wait_send()
             return carry
 
         lax.fori_loop(1, 8, drain, 0)
 
-    return finish
+    return reduce_half, finish
 
 
 def meet():
@@ -343,8 +355,8 @@
 
 
 def cosine_kernel(
-    block, out, paired, times, times_more, freqs, freqs_more, gathered, gathered_more, final, final_more,
-    flat, mirror, mirror_half, joined,
+    reduce_half, out, for_partner, paired, times, times_more, freqs, freqs_more, gathered, gathered_more,
+    final, final_more, flat, mirror, mirror_half, joined,
     swap_send, swap_recv, chip_send, chip_recv, more_send, more_recv, back_send, back_recv,
     back_more_send, back_more_recv, end_send, end_recv, mirror_send, mirror_recv,
 ):
@@ -362,100 +374,130 @@
     def aligned(start, size):
         return pl.ds(pl.multiple_of(start, size), size)
 
-    swap = pltpu.make_async_remote_copy(
-        block.at[aligned((1 - core) * SHARE, SHARE)], paired.at[core], swap_send, swap_recv, device_id=partner,
-    )
+    def wait_bytes(ref, sem):
+        pltpu.make_async_copy(ref, ref, sem).wait()
+
+    swap = pltpu.make_async_remote_copy(for_partner, paired.at[core], swap_send, swap_recv, device_id=partner)
+    reduce_half(1 - core, for_partner)
     swap.start()
-    paired[core] = block[aligned(core * SHARE, SHARE)]
-    swap.wait()
-
-    def more_copy(e):
+
+    def more_copy(which, e):
         return pltpu.make_async_remote_copy(
-            paired.at[:, MAIN + e * 8:MAIN + e * 8 + 8], times_more.at[chip],
-            more_send.at[e], more_recv, device_id=device(5 * e),
-        )
-
-    def spread(i, carry):
-        target = other(i)
-        pltpu.make_async_remote_copy(
-            paired.at[:, aligned(target * 16, 16)], times.at[chip],
-            chip_send, chip_recv, device_id=device(target),
-        ).start()
-        return carry
-
-    lax.fori_loop(1, 16, spread, 0)
-    for e in range(4):
-        @pl.when(chip != 5 * e)
-        def _():
-            more_copy(e).start()
-
-        @pl.when(chip == 5 * e)
-        def _():
-            times_more[chip] = paired[:, MAIN + e * 8:MAIN + e * 8 + 8]
-    times[chip] = paired[:, aligned(chip * 16, 16)]
-    pltpu.make_async_copy(times.at[pl.ds(0, 15)], times.at[pl.ds(0, 15)], chip_recv).wait()
-
-    def transform(source, result, rows):
-        at = [source[t // 2, t % 2, rows] for t in range(32)]
-        mixed = ([at[t] + at[31 - t] for t in range(16)], [at[t] - at[31 - t] for t in range(16)])
-        for freq in range(32):
+            paired.at[which, MAIN + e * 8:MAIN + e * 8 + 8], times_more.at[which, chip],
+            more_send.at[which, e], more_recv.at[which], device_id=device(5 * e),
+        )
+
+    def spread(which):
+        def one(i, carry):
+            target = other(i)
+            pltpu.make_async_remote_copy(
+                paired.at[which, aligned(target * 16, 16)], times.at[which, chip],
+                chip_send.at[which], chip_recv.at[which], device_id=device(target),
+            ).start()
+            return carry
+
+        lax.fori_loop(1, 16, one, 0)
+        for e in range(4):
+            @pl.when(chip != 5 * e)
+            def _():
+                more_copy(which, e).start()
+
+            @pl.when(chip == 5 * e)
+            def _():
+                times_more[which, chip] = paired[which, MAIN + e * 8:MAIN + e * 8 + 8]
+        times[which, chip] = paired[which, aligned(chip * 16, 16)]
+
+    swap.wait_recv()
+    spread(1 - core)
+    reduce_half(core, paired.at[core])
+    spread(core)
+    for which in range(2):
+        wait_bytes(times.at[which, pl.ds(0, 15)], chip_recv.at[which])
+
+    @pl.when(has_more)
+    def _():
+        for which in range(2):
+            wait_bytes(times_more.at[which, pl.ds(0, 15)], more_recv.at[which])
+
+    def transform(source, result, rows, parity):
+        at = [source[t % 2, t // 2, rows] for t in range(32)]
+        if parity:
+            mixed = [at[t] - at[31 - t] for t in range(16)]
+        else:
+            mixed = [at[t] + at[31 - t] for t in range(16)]
+        for freq in range(parity, 32, 2):
             value = None
             for t in range(16):
-                term = cosine(freq, t) * mixed[freq % 2][t]
+                term = cosine(freq, t) * mixed[t]
                 value = term if value is None else value + term
-            result[freq // 2, freq % 2, rows] = value
-
-    def transform_main(i, carry):
-        transform(times, freqs, aligned(i * 8, 8))
-        return carry
-
-    lax.fori_loop(0, 2, transform_main, 0)
-
-    def give(i, carry):
-        target = other(i)
-        pltpu.make_async_remote_copy(
-            freqs.at[target], gathered.at[chip], back_send, back_recv, device_id=device(target),
-        ).start()
-        return carry
-
-    lax.fori_loop(1, 16, give, 0)
-
-    def back_more_copy(target, e):
+            result[parity, freq // 2, rows] = value
+
+    def transform_all(which):
+        for parity in range(2):
+            @pl.when(which == parity)
+            def _():
+                def main(i, carry):
+                    transform(times, freqs, aligned(i * 8, 8), parity)
+                    return carry
+
+                lax.fori_loop(0, 2, main, 0)
+
+                @pl.when(has_more)
+                def _():
+                    transform(times_more, freqs_more, pl.ds(0, 8), parity)
+
+    def back_more_copy(which, target, e):
         return pltpu.make_async_remote_copy(
-            freqs_more.at[target], gathered_more.at[e],
-            back_more_send, back_more_recv.at[e], device_id=device(target),
-        )
-
-    @pl.when(has_more)
-    def _():
-        pltpu.make_async_copy(times_more.at[pl.ds(0, 15)], times_more.at[pl.ds(0, 15)], more_recv).wait()
-        transform(times_more, freqs_more, pl.ds(0, 8))
-
-        def give_more(i, carry):
-            back_more_copy(other(i), lax.div(chip, 5)).start()
-            return carry
-
-        lax.fori_loop(1, 16, give_more, 0)
-        gathered_more[lax.div(chip, 5)] = freqs_more[chip]
-
-    gathered[chip] = freqs[chip]
-    pltpu.make_async_copy(gathered.at[pl.ds(0, 15)], gathered.at[pl.ds(0, 15)], back_recv).wait()
+            freqs_more.at[which, target], gathered_more.at[which, e],
+            back_more_send.at[which], back_more_recv.at[which, e], device_id=device(target),
+        )
+
+    def give(which):
+        def one(i, carry):
+            target = other(i)
+            pltpu.make_async_remote_copy(
+                freqs.at[which, target], gathered.at[which, chip],
+                back_send.at[which], back_recv.at[which], device_id=device(target),
+            ).start()
+            return carry
+
+        lax.fori_loop(1, 16, one, 0)
+
+        @pl.when(has_more)
+        def _():
+            def one_more(i, carry):
+                back_more_copy(which, other(i), lax.div(chip, 5)).start()
+                return carry
+
+            lax.fori_loop(1, 16, one_more, 0)
+            gathered_more[which, lax.div(chip, 5)] = freqs_more[which, chip]
+
+        gathered[which, chip] = freqs[which, chip]
+
+    def take(which):
+        wait_bytes(gathered.at[which, pl.ds(0, 15)], back_recv.at[which])
+        for e in range(4):
+            @pl.when(chip != 5 * e)
+            def _():
+                back_more_copy(which, chip, e).wait_recv()
+
+    for which in (1 - core, core):
+        transform_all(which)
+        give(which)
+    take(1 - core)
     last = pltpu.make_async_remote_copy(
-        gathered.at[:, 1 - core], final.at[core], end_send.at[0], end_recv.at[0], device_id=partner
+        gathered.at[1 - core], final.at[core], end_send.at[0], end_recv.at[0], device_id=partner
+    )
+    last_more = pltpu.make_async_remote_copy(
+        gathered_more.at[1 - core], final_more.at[core], end_send.at[1], end_recv.at[1], device_id=partner
     )
     last.start()
-    for e in range(4):
-        @pl.when(chip != 5 * e)
-        def _():
-            back_more_copy(chip, e).wait_recv()
-    last_more = pltpu.make_async_remote_copy(
-        gathered_more.at[:, 1 - core], final_more.at[core], end_send.at[1], end_recv.at[1], device_id=partner
-    )
     last_more.start()
-    final[core] = gathered[:, core]
-    final_more[core] = gathered_more[:, core]
-    last.wait()
-    last_more.wait()
+    take(core)
+    final[core] = gathered[core]
+    final_more[core] = gathered_more[core]
+    last.wait_recv()
+    last_more.wait_recv()
     for c in range(2):
         for p in range(16):
             flat[c * SHARE + p * 16:c * SHARE + p * 16 + 16] = final[c, p]
@@ -493,31 +535,33 @@
     def _():
         out[0, :, columns(place + 4)] = joined[...].T
 
-    for copy in mirrors:
+    for copy in [*mirrors, swap, last, last_more]:
         copy.wait_send()
-    pltpu.make_async_copy(times.at[pl.ds(0, 15)], times.at[pl.ds(0, 15)], chip_send).wait()
-    pltpu.make_async_copy(times.at[pl.ds(0, 15)], times.at[pl.ds(0, 15)], back_send).wait()
-    for e in range(4):
-        @pl.when(chip != 5 * e)
-        def _():
-            more_copy(e).wait_send()
+    for which in range(2):
+        wait_bytes(times.at[which, pl.ds(0, 15)], chip_send.at[which])
+        wait_bytes(times.at[which, pl.ds(0, 15)], back_send.at[which])
+        for e in range(4):
+            @pl.when(chip != 5 * e)
+            def _():
+                more_copy(which, e).wait_send()
 
     @pl.when(has_more)
     def _():
-        pltpu.make_async_copy(times_more.at[pl.ds(0, 15)], times_more.at[pl.ds(0, 15)], back_more_send).wait()
-
-
-def kernel(occ, vir, eps, out, block, *scratch):
+        for which in range(2):
+            wait_bytes(times_more.at[which, pl.ds(0, 15)], back_more_send.at[which])
+
+
+def kernel(occ, vir, eps, out, *scratch):
     meet()
-    finish = green_kernel(occ, vir, eps, block, *scratch[:GREEN_SCRATCH])
-    cosine_kernel(block, out, *scratch[GREEN_SCRATCH:])
+    reduce_half, finish = green_kernel(occ, vir, eps, *scratch[:GREEN_SCRATCH])
+    cosine_kernel(reduce_half, out, *scratch[GREEN_SCRATCH:])
     finish()
 
 
 def on_device(occ_factor, vir_factor, eps_basis):
     dma = pltpu.SemaphoreType.DMA
-    main = pltpu.VMEM((16, 2, 16, TILE), F32)
-    more = pltpu.VMEM((16, 2, 8, TILE), F32)
+    main = pltpu.VMEM((2, 16, 16, TILE), F32)
+    more = pltpu.VMEM((2, 16, 8, TILE), F32)
     rows_sems = dma((2, 4, len(PARTS)))
     green = [
         pltpu.VMEM((2, 4 * ROWS, 2048), F32),
@@ -533,7 +577,7 @@
         pltpu.VMEM((TILE, 1024), F32),
         pltpu.VMEM((8, KEPT, TILE), F32),
         pltpu.VMEM((8, KEPT, TILE), F32),
-        dma((3,)), dma((4,)), dma((4,)), dma((4, 4)), dma((4, 4)), rows_sems, rows_sems, dma((8,)), dma((8,)),
+        dma((3,)), dma((4,)), dma((4,)), dma((4, 4)), dma((4, 4)), rows_sems, rows_sems, dma((2, 8)), dma((2, 8)),
     ]
     assert len(green) == GREEN_SCRATCH
     return pl.pallas_call(
@@ -542,18 +586,19 @@
         in_specs=[pl.BlockSpec(memory_space=pl.ANY)] * 3,
         out_specs=pl.BlockSpec(memory_space=pltpu.VMEM),
         scratch_shapes=[
-            pltpu.VMEM((KEPT, TILE), F32),
             *green,
+            pltpu.VMEM((SHARE, TILE), F32),
             pltpu.VMEM((2, SHARE, TILE), F32),
             main, more, main, more, main,
-            pltpu.VMEM((4, 2, 8, TILE), F32),
-            pltpu.VMEM((2, 16, 16, TILE), F32),
+            pltpu.VMEM((2, 4, 8, TILE), F32),
+            main,
             pltpu.VMEM((2, 4, 8, TILE), F32),
             pltpu.VMEM((KEPT, TILE), F32),
             pltpu.VMEM((3, TILE, TILE), F32),
             pltpu.VMEM((64, TILE), F32),
             pltpu.VMEM((TILE, TILE), F32),
-            dma, dma, dma, dma, dma((4,)), dma, dma, dma, dma, dma((4,)), dma((2,)), dma((2,)), dma((4,)), dma((4,)),
+            dma, dma, dma((2,)), dma((2,)), dma((2, 4)), dma((2,)), dma((2,)), dma((2,)), dma((2,)), dma((2, 4)), dma((2,)), dma((2,)),
+            dma((4,)), dma((4,)),
         ],
         compiler_params=pltpu.CompilerParams(
             collective_id=0, has_side_effects=True, vmem_limit_bytes=62 << 20

time: 177 us -> 174 us (0.983)
  Pallas kernels: 174 us -> 170 us
    pallas_call x1, Pallas kernels: 174 us -> 170 us  [on_device(): pl.pallas_call(kernel, out_shape=jax.ShapeDtypeStruct((1, TILE, 1024), F3...]
where the time goes in v5:
time: 174 us; the launch traced here: 172 us
  Pallas kernels  170 us (98%)
  local copies, waits for them, and re-layouts  1.89 us (1%)
    pallas_call x1, Pallas kernels, on_device(): pl.pallas_call(kernel, out_shape=jax.ShapeDtypeStruct((1, TILE, 1024), F3...  170 us

profile of v5, /device:TPU:1, one launch (start us, length us, event | category | flops | bytes accessed | tf_op | source)
XLA Modules:
  0.0 172.1 jit_solution(6936089239284232708)
XLA Ops:
  0.0 170.2 %polarizability.1 = f32[1,128,1024]{2,1,0:T(8,128)} custom-call(f32[1,256,2048]{2,1,0:T(8,128)} %occ.1, f32[1,256,2048]{2,1,0:T(8,128)} %vir.1, f32[256,1024]{1,0:T(8,128)} %eps.1), custom_call_target="tpu_custom_call" | custom-call | flops 20000000000 | bytes 20971520 | tf_op jit(solution)/shard_map/polarizability/pallas_call | solution.py:583
  170.2 1.9 %copy.5 = f32[1,128,1024]{2,1,0:T(8,128)} copy(f32[1,128,1024]{2,1,0:T(8,128)} %polarizability.1) | data formatting | bytes 1048576

commit v6 on v5

--- a/solution.py
+++ b/solution.py
@@ -23,7 +23,7 @@
 KEPT = 4 * TILE + 64
 SHARE = KEPT // 2
 MAIN = 256
-GREEN_SCRATCH = 22
+GREEN_SCRATCH = 24
 
 
 def ring_place(row):
@@ -49,7 +49,7 @@
 
 def green_kernel(
     occ, vir, eps, full, high, low, basis, basis_high, basis_low, polar, late, late_basis, total, turned, staged, arrived,
-    local_sem, basis_send, basis_recv, share_send, share_recv, send, recv, part_send, part_recv,
+    local_sem, basis_send, basis_recv, share_send, share_recv, cross_send, cross_recv, send, recv, part_send, part_recv,
 ):
     row, tm = lax.axis_index("row"), lax.axis_index("tm")
     y, z = lax.div(row, 2), lax.rem(row, 2)
@@ -64,26 +64,45 @@
             return pl.ds(slot * ROWS, ROWS)
         return pl.ds(slot * ROWS + PARTS[chunk][0], PARTS[chunk][1])
 
-    def quarter(slot, of):
-        return pl.ds(pl.multiple_of(slot * ROWS + of * QUARTER, QUARTER), QUARTER)
+    core = lax.rem(tm, 2)
+    other_core = {"row": row, "tm": tm + 1 - 2 * core}
+
+    def piece(slot, of, alone):
+        if alone:
+            return pl.ds(pl.multiple_of(slot * ROWS + of * QUARTER, QUARTER), QUARTER)
+        return pl.ds(pl.multiple_of(slot * ROWS + of * QUARTER + core * (QUARTER // 2), QUARTER // 2), QUARTER // 2)
 
     def send_basis(src, slot, device):
         return pltpu.make_async_remote_copy(
-            src, basis.at[quarter(slot, x)], basis_send.at[slot], basis_recv.at[slot], device_id=device
+            src, basis.at[piece(slot, x, slot == NEXT)], basis_send.at[slot], basis_recv.at[slot], device_id=device
         )
 
     def share_basis(slot):
         copies["basis", slot].wait_recv()
-        part = basis.at[quarter(slot, x)]
+        part = basis.at[piece(slot, x, slot == NEXT)]
         for i in range(1, 4):
             copies["share", slot, i] = pltpu.make_async_remote_copy(
                 part, part, share_send.at[slot, i], share_recv.at[slot, i], device_id=beside[i]
             )
             copies["share", slot, i].start()
 
-    def take_basis(slot):
+    def cross_basis(slot):
         for i in range(1, 4):
             copies["share", slot, i].wait_recv()
+        for of in range(4):
+            part = basis.at[piece(slot, of, False)]
+            copies["cross", slot, of] = pltpu.make_async_remote_copy(
+                part, part, cross_send.at[slot, of], cross_recv.at[slot, of], device_id=other_core
+            )
+            copies["cross", slot, of].start()
+
+    def take_basis(slot):
+        if slot == NEXT:
+            for i in range(1, 4):
+                copies["share", slot, i].wait_recv()
+        else:
+            for of in range(4):
+                copies["cross", slot, of].wait_recv()
         convert_basis(slot)
 
     def send_rows(which, chunk, src, slot, device):
@@ -94,8 +113,8 @@
 
     sources = (occ.at[0], vir.at[0])
     copies = {}
-    copies["basis", NEXT] = send_basis(eps.at[quarter(0, x)], NEXT, before)
-    copies["basis", ACROSS] = send_basis(eps.at[quarter(0, x)], ACROSS, across)
+    copies["basis", NEXT] = send_basis(eps.at[piece(0, x, True)], NEXT, before)
+    copies["basis", ACROSS] = send_basis(eps.at[piece(0, x, False)], ACROSS, across)
     for chunk in range(len(PARTS)):
         for which in range(2):
             part = sources[which].at[pl.ds(*PARTS[chunk])]
@@ -224,7 +243,7 @@
 
     convert_basis(OWN)
     share_basis(NEXT)
-    copies["basis", FAR] = send_basis(basis.at[quarter(NEXT, x)], FAR, before)
+    copies["basis", FAR] = send_basis(basis.at[piece(NEXT, x, False)], FAR, before)
     copies["basis", FAR].start()
     share_basis(ACROSS)
     convert(OWN, 0, ROWS)
@@ -236,11 +255,13 @@
             copies[which, FAR, chunk] = send_rows(which, chunk, full.at[which, block(NEXT, chunk)], FAR, before)
             copies[which, FAR, chunk].start()
     share_basis(FAR)
+    cross_basis(ACROSS)
     take_basis(NEXT)
     convert(NEXT, 0, ROWS)
     work(NEXT, 0, 128, [(at(OWN), ROWS, 1.0)])
     work(NEXT, 128, 128, [(at(OWN), ROWS, 1.0)])
 
+    cross_basis(FAR)
     take_basis(ACROSS)
     take_basis(FAR)
     prepare_late_basis()
@@ -274,8 +295,6 @@
             total[half, span(high_tile)] + turned[pl.ds(pl.multiple_of(upper * 64, 64), 64), 0:TILE]
         )
 
-    core = lax.rem(tm, 2)
-
     def half_rows(half):
         return pl.ds(pl.multiple_of(half * SHARE, SHARE), SHARE)
 
@@ -493,36 +512,47 @@
     )
     last.start()
     last_more.start()
+    place = ring_place(row)
+    pieces = (((128, 128, 1), (256, 32, 2)), ((288, 96, 2), (384, 128, 3), (512, 64, 4)))
+    mirrors = [], []
+    for half in range(2):
+        for start, count, d in pieces[half]:
+            to = mirror_half if d == 4 else mirror.at[d - 1, pl.ds(start - d * TILE, count)]
+            k = len(mirrors[0]) + len(mirrors[1])
+            mirrors[half].append(pltpu.make_async_remote_copy(
+                flat.at[pl.ds(start, count)], to, mirror_send.at[k], mirror_recv.at[k],
+                device_id={"row": ring_row(place + d), "tm": tm},
+            ))
+
+    def complete(half):
+        for p in range(16):
+            flat[aligned(half * SHARE + p * 16, 16)] = final[half, p]
+        for e in range(4):
+            flat[aligned(half * SHARE + MAIN + e * 8, 8)] = final_more[half, e]
+        for known in range(2):
+            @pl.when(half == known)
+            def _():
+                for copy in mirrors[known]:
+                    copy.start()
+
+    last.wait_recv()
+    last_more.wait_recv()
+    complete(1 - core)
     take(core)
     final[core] = gathered[core]
     final_more[core] = gathered_more[core]
-    last.wait_recv()
-    last_more.wait_recv()
-    for c in range(2):
-        for p in range(16):
-            flat[c * SHARE + p * 16:c * SHARE + p * 16 + 16] = final[c, p]
-        for e in range(4):
-            flat[c * SHARE + MAIN + e * 8:c * SHARE + MAIN + e * 8 + 8] = final_more[c, e]
-
-    mirrors = []
-    place = ring_place(row)
-    for d in range(1, 5):
-        part, to = (pl.ds(d * TILE, TILE), mirror.at[d - 1]) if d < 4 else (pl.ds(4 * TILE, 64), mirror_half)
-        mirrors.append(pltpu.make_async_remote_copy(
-            flat.at[part], to, mirror_send.at[d - 1], mirror_recv.at[d - 1],
-            device_id={"row": ring_row(place + d), "tm": tm},
-        ))
-        mirrors[-1].start()
+    complete(core)
 
     def columns(j):
         return aligned(ring_row(j) * TILE, TILE)
 
     for d in range(4):
         out[0, :, columns(place + d)] = flat[d * TILE:(d + 1) * TILE]
+    for half in range(2):
+        for copy in mirrors[half]:
+            copy.wait_recv()
     for d in range(1, 4):
-        mirrors[d - 1].wait_recv()
         out[0, :, columns(place + 8 - d)] = mirror[d - 1].T
-    mirrors[3].wait_recv()
     upper = lax.div(place, 4)
     joined[aligned(upper * 64, 64)] = flat[4 * TILE:KEPT]
     joined[aligned((1 - upper) * 64, 64)] = mirror_half[...]
@@ -535,7 +565,7 @@
     def _():
         out[0, :, columns(place + 4)] = joined[...].T
 
-    for copy in [*mirrors, swap, last, last_more]:
+    for copy in [*mirrors[0], *mirrors[1], swap, last, last_more]:
         copy.wait_send()
     for which in range(2):
         wait_bytes(times.at[which, pl.ds(0, 15)], chip_send.at[which])
@@ -577,7 +607,7 @@
         pltpu.VMEM((TILE, 1024), F32),
         pltpu.VMEM((8, KEPT, TILE), F32),
         pltpu.VMEM((8, KEPT, TILE), F32),
-        dma((3,)), dma((4,)), dma((4,)), dma((4, 4)), dma((4, 4)), rows_sems, rows_sems, dma((2, 8)), dma((2, 8)),
+        dma((3,)), dma((4,)), dma((4,)), dma((4, 4)), dma((4, 4)), dma((4, 4)), dma((4, 4)), rows_sems, rows_sems, dma((2, 8)), dma((2, 8)),
     ]
     assert len(green) == GREEN_SCRATCH
     return pl.pallas_call(
@@ -598,10 +628,10 @@
             pltpu.VMEM((64, TILE), F32),
             pltpu.VMEM((TILE, TILE), F32),
             dma, dma, dma((2,)), dma((2,)), dma((2, 4)), dma((2,)), dma((2,)), dma((2,)), dma((2,)), dma((2, 4)), dma((2,)), dma((2,)),
-            dma((4,)), dma((4,)),
+            dma((5,)), dma((5,)),
         ],
         compiler_params=pltpu.CompilerParams(
-            collective_id=0, has_side_effects=True, vmem_limit_bytes=62 << 20
+            collective_id=0, has_side_effects=True, vmem_limit_bytes=59 << 20
         ),
         cost_estimate=pl.CostEstimate(flops=20 * 10**9, bytes_accessed=20 << 20, transcendentals=0),
         name="polarizability",

time: 174 us -> 173 us (level)
  no operation moved by 1% of the time
where the time goes in v6:
time: 173 us; the launch traced here: 171 us
  Pallas kernels  169 us (98%)
  local copies, waits for them, and re-layouts  1.89 us (1%)
    pallas_call x1, Pallas kernels, on_device(): pl.pallas_call(kernel, out_shape=jax.ShapeDtypeStruct((1, TILE, 1024), F3...  169 us

profile of v6, /device:TPU:1, one launch (start us, length us, event | category | flops | bytes accessed | tf_op | source)
XLA Modules:
  0.0 170.7 jit_solution(8835471745306629566)
XLA Ops:
  0.0 168.8 %polarizability.1 = f32[1,128,1024]{2,1,0:T(8,128)} custom-call(f32[1,256,2048]{2,1,0:T(8,128)} %occ.1, f32[1,256,2048]{2,1,0:T(8,128)} %vir.1, f32[256,1024]{1,0:T(8,128)} %eps.1), custom_call_target="tpu_custom_call" | custom-call | flops 20000000000 | bytes 20971520 | tf_op jit(solution)/shard_map/polarizability/pallas_call | solution.py:613
  168.8 1.9 %copy.5 = f32[1,128,1024]{2,1,0:T(8,128)} copy(f32[1,128,1024]{2,1,0:T(8,128)} %polarizability.1) | data formatting | bytes 1048576

commit v7 on v6

--- a/solution.py
+++ b/solution.py
@@ -278,22 +278,34 @@
     convert_late(1, FAR)
     late_work()
 
-    def fold(owner, slot):
+    def fold(owner, slot, half):
         def span(j):
             return pl.ds(pl.multiple_of(j * TILE, TILE), TILE)
 
         rows = span(owner)
         place = ring_place(owner)
-        for d in range(4):
+
+        def tile_of(d):
             tile = span(ring_row(place + d))
-            staged[slot, d * TILE:(d + 1) * TILE] = total[rows, tile] + total[tile, rows].T
-        upper = lax.div(place, 4)
-        low_tile, high_tile = ring_row(lax.rem(place, 4)), ring_row(lax.rem(place, 4) + 4)
-        turned[:, 0:TILE] = total[span(high_tile), span(low_tile)].T
-        half = pl.ds(pl.multiple_of(low_tile * TILE + upper * 64, 64), 64)
-        staged[slot, 4 * TILE:KEPT] = (
-            total[half, span(high_tile)] + turned[pl.ds(pl.multiple_of(upper * 64, 64), 64), 0:TILE]
-        )
+            return total[rows, tile] + total[tile, rows].T
+
+        @pl.when(half == 0)
+        def _():
+            for d in range(2):
+                staged[slot, d * TILE:(d + 1) * TILE] = tile_of(d)
+            staged[slot, 2 * TILE:SHARE] = tile_of(2)[0:SHARE - 2 * TILE]
+
+        @pl.when(half == 1)
+        def _():
+            staged[slot, SHARE:3 * TILE] = tile_of(2)[SHARE - 2 * TILE:]
+            staged[slot, 3 * TILE:4 * TILE] = tile_of(3)
+            upper = lax.div(place, 4)
+            low_tile, high_tile = ring_row(lax.rem(place, 4)), ring_row(lax.rem(place, 4) + 4)
+            turned[:, 0:TILE] = total[span(high_tile), span(low_tile)].T
+            rows_64 = pl.ds(pl.multiple_of(low_tile * TILE + upper * 64, 64), 64)
+            staged[slot, 4 * TILE:KEPT] = (
+                total[rows_64, span(high_tile)] + turned[pl.ds(pl.multiple_of(upper * 64, 64), 64), 0:TILE]
+            )
 
     def half_rows(half):
         return pl.ds(pl.multiple_of(half * SHARE, SHARE), SHARE)
@@ -306,17 +318,20 @@
 
     def send_first(i, carry):
         owner = lax.rem(row + i, 8)
-        fold(owner, i)
+        fold(owner, i, 1 - core)
         part_copy(owner, i, 1 - core).start()
         return carry
 
     def send_second(i, carry):
-        part_copy(lax.rem(row + i, 8), i, core).start()
+        owner = lax.rem(row + i, 8)
+        fold(owner, i, core)
+        part_copy(owner, i, core).start()
         return carry
 
     lax.fori_loop(1, 8, send_first, 0)
     lax.fori_loop(1, 8, send_second, 0)
-    fold(row, 0)
+    fold(row, 0, 1 - core)
+    fold(row, 0, core)
 
     def reduce_half(half, result):
         def take_part(i, carry):

time: 173 us -> 173 us (level)
  no operation moved by 1% of the time
where the time goes in v7:
time: 173 us; the launch traced here: 171 us
  Pallas kernels  169 us (98%)
  local copies, waits for them, and re-layouts  1.89 us (1%)
    pallas_call x1, Pallas kernels, on_device(): pl.pallas_call(kernel, out_shape=jax.ShapeDtypeStruct((1, TILE, 1024), F3...  169 us

profile of v7, /device:TPU:1, one launch (start us, length us, event | category | flops | bytes accessed | tf_op | source)
XLA Modules:
  0.0 171.1 jit_solution(9041285429718025127)
XLA Ops:
  0.0 169.2 %polarizability.1 = f32[1,128,1024]{2,1,0:T(8,128)} custom-call(f32[1,256,2048]{2,1,0:T(8,128)} %occ.1, f32[1,256,2048]{2,1,0:T(8,128)} %vir.1, f32[256,1024]{1,0:T(8,128)} %eps.1), custom_call_target="tpu_custom_call" | custom-call | flops 20000000000 | bytes 20971520 | tf_op jit(solution)/shard_map/polarizability/pallas_call | solution.py:628
  169.2 1.9 %copy.5 = f32[1,128,1024]{2,1,0:T(8,128)} copy(f32[1,128,1024]{2,1,0:T(8,128)} %polarizability.1) | data formatting | bytes 1048576
